TPU v7x, 512 devices: a whole 4x4x16 slice. The times are simulated.
512 devices in a mesh: lang: 16 (over z), dp: 4 (over y), fsdp: 8 (over x, core).
Axes of the slice: x: 4, y: 4, z: 16, core: 2. Of those that a mesh axis runs over, the one named last changes fastest.
Arguments:
- tokens: bfloat16 [16, 1536, 2048], P('lang', ('dp', 'fsdp')), may hold values from -48 to 48
- cotangent: bfloat16 [16, 1536, 2048], P('lang', ('dp', 'fsdp')), may hold values from -48 to 48
- lengths: int32 [16, 12], P('lang'), may hold values from 32 to 128
- up_weight: bfloat16 [2048, 8192], P(None, ('dp', 'fsdp')), may hold values from -0.125 to 0.125
- down_weight: bfloat16 [8192, 2048], P(('dp', 'fsdp')), may hold values from -0.0625 to 0.0625
- targets: float32 [16, 16], replicated, may hold values from 0 to 0.5
- accept: int32 [16, 16], replicated, may hold values 0 or 1
Outputs:
- up_update: float32 [2048, 8192], P('lang', ('dp', 'fsdp'))
- down_update: float32 [8192, 2048], P(('dp', 'fsdp'), 'lang')
- new_targets: float32 [16, 16], replicated
All inputs are finite; a program needn't handle non-finite values.
Results may differ from a plain program's by a relative error of at most 0.0065.
Values may be sent and summed in bfloat16 or wider, within the bound.
A program may use at most 64 MiB of HBM per device.

v0:
```python
import jax
import jax.numpy as jnp
from jax import lax
from jax.sharding import PartitionSpec as P

D = 2048
FF = 8192
SEQ = 128


ema_rate = 0.01
clip_level = 0.25


def gelu_tanh(values):
    return jax.nn.gelu(values, approximate=True)


def token_grads(inputs, upstream, seq_lengths, w_up, w_down):
    row_count = inputs.shape[0]
    row_index = jnp.arange(row_count, dtype=jnp.int32)
    seq_of = row_index // SEQ
    position = row_index % SEQ
    chosen = (seq_of[:, None] == jnp.arange(seq_lengths.shape[0], dtype=jnp.int32)[None, :]).astype(
        jnp.int32
    )
    seq_limit = jnp.sum(chosen * seq_lengths[None, :], axis=1)
    keep_mask = (position < seq_limit).astype(upstream.dtype)
    masked = upstream * keep_mask[:, None]
    preact = jnp.dot(inputs, w_up, preferred_element_type=jnp.float32)
    hidden, backward = jax.vjp(gelu_tanh, preact)
    hidden = hidden.astype(jnp.bfloat16)
    hidden_grad = lax.dot_general(
        masked, w_down, (((1,), (1,)), ((), ())), preferred_element_type=jnp.float32
    )
    preact_grad = backward(hidden_grad)[0].astype(jnp.bfloat16)
    g_up = lax.dot_general(
        inputs, preact_grad, (((0,), (0,)), ((), ())), preferred_element_type=jnp.float32
    )
    g_dt = lax.dot_general(
        masked, hidden, (((0,), (0,)), ((), ())), preferred_element_type=jnp.float32
    )
    return (g_up, g_dt)


def vaccinate(gram_sums, targets, accept):
    groups = gram_sums.shape[0]
    identity = jnp.eye(groups, dtype=jnp.float32)
    diagonal = jnp.diagonal(gram_sums)
    cos_pairs = gram_sums / jnp.sqrt(diagonal[:, None] * diagonal[None, :])
    allowed = accept.astype(jnp.float32) * (1.0 - identity)
    target_roots = jnp.sqrt(1.0 - targets * targets)
    high = lax.Precision.HIGHEST

    def project(target, coeffs):
        onehot = (jnp.arange(groups, dtype=jnp.int32) == target).astype(jnp.float32)
        column = jnp.dot(gram_sums, onehot, precision=high)
        inner_prod = jnp.dot(coeffs, column, precision=high)
        norm_sq = jnp.sum(jnp.dot(coeffs, gram_sums, precision=high) * coeffs, axis=1)
        own_norm = jnp.dot(column, onehot, precision=high)
        cosine = inner_prod / jnp.sqrt(norm_sq * own_norm)
        target_col = jnp.dot(targets, onehot, precision=high)
        target_root = jnp.dot(target_roots, onehot, precision=high)
        gate_col = jnp.dot(allowed, onehot, precision=high)
        sine = jnp.sqrt(jnp.maximum(1.0 - cosine * cosine, 0.0))
        step_size = (
            jnp.sqrt(norm_sq)
            * (target_col * sine - cosine * target_root)
            / (jnp.sqrt(own_norm) * target_root)
        )
        applied = jnp.where(gate_col > 0.5, step_size, 0.0)
        return coeffs + applied[:, None] * onehot[None, :]

    coeffs = lax.fori_loop(0, groups, project, identity)
    weights = jnp.sum(coeffs, axis=0)
    new_targets = (1.0 - ema_rate) * targets + ema_rate * cos_pairs
    return (weights, new_targets)


def on_device(tokens, cotangent, lengths, up_weight, down_weight, targets, accept):
    seq_lengths = lengths[0]
    all_inputs, all_upstream = (
        lax.all_gather(tokens, ("dp", "fsdp"), axis=1, tiled=True),
        lax.all_gather(cotangent, ("dp", "fsdp"), axis=1, tiled=True),
    )
    g_up, g_dt = token_grads(all_inputs[0], all_upstream[0], seq_lengths, up_weight, down_weight)
    outgoing = (g_up.astype(jnp.bfloat16)[None], g_dt.astype(jnp.bfloat16)[None])
    part_up, part_dt = (
        lax.all_to_all(outgoing[0], "lang", split_axis=1, concat_axis=0, tiled=True),
        lax.all_to_all(outgoing[1], "lang", split_axis=1, concat_axis=0, tiled=True),
    )
    partial_value = lax.dot_general(
        part_up, part_up, (((1, 2), (1, 2)), ((), ())), preferred_element_type=jnp.float32
    )
    partial_value = partial_value + lax.dot_general(
        part_dt, part_dt, (((1, 2), (1, 2)), ((), ())), preferred_element_type=jnp.float32
    )
    gram_sums = lax.psum(partial_value, ("lang", "dp", "fsdp"))
    weights, new_targets = vaccinate(gram_sums, targets, accept)
    combined_up = jnp.einsum("l,lij->ij", weights, part_up.astype(jnp.float32))
    combined_dt = jnp.einsum("l,lij->ij", weights, part_dt.astype(jnp.float32))
    local_sum = jnp.sum(combined_up * combined_up) + jnp.sum(combined_dt * combined_dt)
    mean_square = lax.psum(local_sum, ("lang", "dp", "fsdp")) / (2.0 * D * FF)
    factor = jnp.minimum(1.0, clip_level / jnp.sqrt(mean_square + 1e-06))
    return (factor * combined_up, (factor * combined_dt).T, new_targets)


def solution(mesh):
    in_specs = (
        P("lang", ("dp", "fsdp"), None),
        P("lang", ("dp", "fsdp"), None),
        P("lang", None),
        P(None, ("dp", "fsdp")),
        P(("dp", "fsdp"), None),
        P(),
        P(),
    )
    out_specs = (P("lang", ("dp", "fsdp")), P(("dp", "fsdp"), "lang"), P())
    return jax.shard_map(
        on_device, mesh=mesh, in_specs=in_specs, out_specs=out_specs, check_vma=False
    )
```

profile of v0, /device:TPU:1, one launch (start us, length us, event | category | flops | bytes accessed | tf_op | source)
XLA Modules:
  0.0 570.9 jit_solution(4176614109579149993)
XLA Ops:
  9.4 71.9 %all-gather.5.cloned.1.call-done = bf16[1,1536,2048]{2,1,0:T(8,128)(2,1)} async-done(((bf16[1,48,2048]{2,1,0:T(8,128)(2,1)}), bf16[1,1536,2048]{2,1,0:T(8,128)(2,1)}) %all-gather.5.cloned.1.call-update) | async-done | bytes 6291472 | tf_op jit(solution)/shard_map/all_gather | solution.py:83
  81.3 4.8 fusion.21
  86.2 61.8 %all-gather.3.cloned.1.call-done = bf16[1,1536,2048]{2,1,0:T(8,128)(2,1)} async-done(((bf16[1,48,2048]{2,1,0:T(8,128)(2,1)}), bf16[1,1536,2048]{2,1,0:T(8,128)(2,1)}) %all-gather.3.cloned.1.call-update) | async-done | bytes 6291472 | tf_op jit(solution)/shard_map/all_gather | solution.py:84
  148.0 12.9 %fusion.32 = bf16[1,2048,256]{1,2,0:T(8,128)(2,1)} fusion(bf16[1,1536,2048]{2,1,0:T(8,128)(2,1)} %all-gather.5.cloned.1.call-done, f32[1536,256]{1,0:T(8,128)S(1)} %fusion.21, bf16[256,2048]{1,0:T(8,128)(2,1)S(1)} %copy-done, bf16[1,1536,2048]{2,1,0:T(8,128)(2,1)} %all-gather.3.cloned.1.call-done, bf16[1536]{0:T(1024)(128)(2,1)S(1)} %fusion.65), kind=kOutput, calls=%fused_computation.40 | convolution fusion | flops 3232759808 | bytes 16256000 | tf_op jit(solution)/shard_map/dot_general | solution.py:37
  160.9 4.6 copy.35
  166.0 11.6 %reduce.2 = bf16[2048,256]{1,0:T(8,128)(2,1)} reduce(bf16[2048,1,256]{2,1,0:T(2,128)(2,1)S(1)} %bitcast.151, bf16[]{:T(256)} %broadcast.170), dimensions={1}, to_apply=%bitcast.95.reduce_sub_computation | reduce | bytes 2097154
  177.6 2.1 reshape.72
  179.8 12.2 %all-to-all-start = ((bf16[16,2,16384]{2,1,0:T(2,128)(2,1)}), bf16[16,2,16384]{2,1,0:T(2,128)(2,1)}, u32[]{:S(2)}, u32[]{:S(2)}) async-start(bf16[16,2,16384]{2,1,0:T(2,128)(2,1)} %reshape.72), calls=%async_computation | async-start | bytes 2097152 | tf_op jit(solution)/shard_map/all_to_all | solution.py:89
  192.0 5.2 fusion.31
  197.2 11.7 %copy.53 = bf16[1,2048,256]{2,0,1:T(2,128)(2,1)S(1)} copy(bf16[1,2048,256]{2,1,0:T(8,128)(2,1)S(1)} %fusion.31) | data formatting | bytes 2097152 | tf_op jit(solution)/shard_map/broadcast_in_dim | solution.py:87
  209.0 11.6 %reduce.3 = bf16[2048,256]{1,0:T(8,128)(2,1)} reduce(bf16[2048,1,256]{2,1,0:T(2,128)(2,1)S(1)} %bitcast.152, bf16[]{:T(256)} %broadcast.170), dimensions={1}, to_apply=%bitcast.114.reduce_sub_computation | reduce | bytes 2097154
  220.6 2.2 reshape.74
  222.8 15.1 %all-to-all-done = bf16[16,2,16384]{2,1,0:T(2,128)(2,1)} async-done(((bf16[16,2,16384]{2,1,0:T(2,128)(2,1)}), bf16[16,2,16384]{2,1,0:T(2,128)(2,1)}, u32[]{:S(2)}, u32[]{:S(2)}) %all-to-all-start) | async-done | bytes 1048608 | tf_op jit(solution)/shard_map/all_to_all | solution.py:89
  237.9 12.2 %all-to-all-start.1 = ((bf16[16,2,16384]{2,1,0:T(2,128)(2,1)}), bf16[16,2,16384]{2,1,0:T(2,128)(2,1)}, u32[]{:S(2)}, u32[]{:S(2)}) async-start(bf16[16,2,16384]{2,1,0:T(2,128)(2,1)} %reshape.74), calls=%async_computation.1 | async-start | bytes 2097152 | tf_op jit(solution)/shard_map/all_to_all | solution.py:90
  250.2 4.3 reshape.73
  254.6 1.2 copy.46
  255.8 1.9 copy.45
  257.7 37.6 %all-to-all-done.1 = bf16[16,2,16384]{2,1,0:T(2,128)(2,1)} async-done(((bf16[16,2,16384]{2,1,0:T(2,128)(2,1)}), bf16[16,2,16384]{2,1,0:T(2,128)(2,1)}, u32[]{:S(2)}, u32[]{:S(2)}) %all-to-all-start.1) | async-done | bytes 1048608 | tf_op jit(solution)/shard_map/all_to_all | solution.py:90
  295.4 5.8 %reshape.75 = bf16[2048,1,256]{2,1,0:T(2,128)(2,1)} reshape(bf16[16,2,16384]{2,1,0:T(2,128)(2,1)} %all-to-all-done.1) | data formatting | bytes 2097152
  301.1 1.8 copy.47
  304.0 108.6 %psum.14 = f32[16,16]{1,0:T(8,128)S(1)} all-reduce(f32[16,16]{1,0:T(8,128)S(1)} %fusion.42), channel_id=1, replica_groups=mesh['lang'=16,'dp'=4,'fsdp'=8] {'lang','dp','fsdp'}, use_global_device_ids=true, to_apply=%region_1.2 | all-reduce | flops 256 | bytes 2048 | tf_op jit(solution)/shard_map/psum | solution.py:98
  413.9 46.6 %while.13 = (s32[]{:T(128)}, f32[16,16]{0,1:T(8,128)S(1)}, f32[16,16]{1,0:T(8,128)S(1)}, f32[16,16]{1,0:T(8,128)S(1)}, f32[16,16]{1,0:T(8,128)S(1)}, /*index=5*/f32[16,16]{1,0:T(8,128)S(1)}, s32[]{:T(128)}) while((s32[]{:T(128)}, f32[16,16]{0,1:T(8,128)S(1)}, f32[16,16]{1,0:T(8,128)S(1)}, f32[16,16]{1,0:T(8,128)S(1)}, f32[16,16]{1,0:T(8,128)S(1)}, ...), condition=%wide.region_4.5_spmd, body=%wide.region_2.4_spmd.sunk | while | flops 65873 | bytes 10293 | solution.py:74
  423.6 0.8 fusion.120
  463.6 98.3 %psum.15 = f32[]{:T(128)} all-reduce(f32[]{:T(128)S(6)} %add.69), channel_id=1, replica_groups=mesh['lang'=16,'dp'=4,'fsdp'=8] {'lang','dp','fsdp'}, use_global_device_ids=true, to_apply=%region_8.9 | all-reduce | flops 1 | bytes 8 | tf_op jit(solution)/shard_map/psum | solution.py:103
  (161 shorter events, 43.0 us)
Async XLA Ops:
  7.2 140.9 %copy-start = (bf16[256,2048]{1,0:T(8,128)(2,1)S(1)}, bf16[256,2048]{1,0:T(8,128)(2,1)}, u32[]{:S(2)}) copy-start(bf16[256,2048]{1,0:T(8,128)(2,1)} %param.13) | copy-start | bytes 3145732
  7.2 74.2 %all-gather.5.cloned.1.call-start = ((), (), s32[]{:S(2)}) async-start(), calls=%async_computation.3 | async-start | bytes 6488064 | tf_op jit(solution)/shard_map/all_gather | solution.py:83
  7.9 140.1 %all-gather.3.cloned.1.call-start = ((), (), s32[]{:S(2)}) async-start(), calls=%async_computation.2 | async-start | bytes 6488064 | tf_op jit(solution)/shard_map/all_gather | solution.py:84
  86.2 61.8 %copy-start.3 = (f32[1536,256]{1,0:T(8,128)}, f32[1536,256]{1,0:T(8,128)S(1)}, u32[]{:S(2)}) copy-start(f32[1536,256]{1,0:T(8,128)S(1)} %fusion.21) | copy-start | bytes 4718596
  179.8 12.2 %copy-start.4 = (f32[1536,256]{1,0:T(8,128)S(1)}, f32[1536,256]{1,0:T(8,128)}, u32[]{:S(2)}) copy-start(f32[1536,256]{1,0:T(8,128)} %copy-done.3) | copy-start | bytes 4718596
  179.8 58.1 %all-to-all-start = ((bf16[16,2,16384]{2,1,0:T(2,128)(2,1)}), bf16[16,2,16384]{2,1,0:T(2,128)(2,1)}, u32[]{:S(2)}, u32[]{:S(2)}) async-start(bf16[16,2,16384]{2,1,0:T(2,128)(2,1)} %reshape.72), calls=%async_computation | async-start | bytes 2097152 | tf_op jit(solution)/shard_map/all_to_all | solution.py:89
  222.8 27.4 %copy-start.1 = (s32[16,16]{1,0:T(8,128)S(1)}, s32[16,16]{1,0:T(8,128)}, u32[]{:S(2)}) copy-start(s32[16,16]{1,0:T(8,128)} %param.15) | copy-start | bytes 3076
  237.9 57.4 %all-to-all-start.1 = ((bf16[16,2,16384]{2,1,0:T(2,128)(2,1)}), bf16[16,2,16384]{2,1,0:T(2,128)(2,1)}, u32[]{:S(2)}, u32[]{:S(2)}) async-start(bf16[16,2,16384]{2,1,0:T(2,128)(2,1)} %reshape.74), calls=%async_computation.1 | async-start | bytes 2097152 | tf_op jit(solution)/shard_map/all_to_all | solution.py:90
  303.6 109.7 %copy-start.2 = (f32[16,16]{1,0:T(8,128)S(1)}, f32[16,16]{1,0:T(8,128)}, u32[]{:S(2)}) copy-start(f32[16,16]{1,0:T(8,128)} %param.14) | copy-start | bytes 3076
Sparse Core Ops, SparseCore 0:
  11.1 70.1 all-gather.4
  84.5 63.5 all-gather.2
where the time goes:
time: 572 us; the launch traced here: 571 us
  blocking collectives  207 us (36%)
  waiting for transfers between devices  188 us (33%)
  matrix products  58.7 us (10%)
  local copies, waits for them, and re-layouts  37.8 us (7%)
  other arithmetic  27.7 us (5%)
  starting transfers between devices  24.5 us (4%)
  between operations  16.2 us (3%)
  loops' own time  11.3 us (2%)
    psum x1, blocking collectives, on_device(): gram_sums = lax.psum(partial_value, ('lang', 'dp', 'fsdp'))  109 us
    psum x1, blocking collectives, on_device(): mean_square = lax.psum(local_sum, ('lang', 'dp', 'fsdp')) / (2.0 * D * FF)  98.3 us
    all_gather x1, waiting for transfers between devices, on_device(): lax.all_gather(tokens, ('dp', 'fsdp'), axis=1, tiled=True)  71.9 us
    all_gather x1, waiting for transfers between devices, on_device(): lax.all_gather(cotangent, ('dp', 'fsdp'), axis=1, tiled=True)  61.8 us
    all_to_all x1, waiting for transfers between devices, on_device(): lax.all_to_all(outgoing[1], 'lang', split_axis=1, concat_axis=0, tiled=True)  37.6 us
    unnamed x2, other arithmetic  23.2 us
    unnamed x18, local copies, waits for them, and re-layouts  18.7 us
    all_to_all x1, waiting for transfers between devices, on_device(): lax.all_to_all(outgoing[0], 'lang', split_axis=1, concat_axis=0, tiled=True)  15.1 us
  transfers between devices with their start and end apart: 4, of which 4 were waited for; matrix products, arithmetic and copies ran while one was open for 8% of the time, Pallas kernels for 0%

commit v1 on v0

v1 whole, which is shorter than its diff:
```python
import functools

import jax
import jax.numpy as jnp
from jax import lax
from jax.experimental import pallas as pl
from jax.experimental.pallas import tpu as pltpu
from jax.sharding import PartitionSpec as P

D = 2048
FF = 8192
SEQ = 128
LTOK = 1536
LANGS = 16
NY = 4
NX = 4
NF = 8
ROWS = 48
HID = 256
DS = 128
HALF = D // 2

ema_rate = 0.01
clip_level = 0.25
MESH = pl.DeviceIdType.MESH

OFFSETS = (0, 3, 1, 2)
ARRIVALS = (
    (0, 1), (0, 2), (1, 0), (2, 0), (0, 3), (1, 1), (2, 1), (1, 2), (2, 2),
    (3, 0), (1, 3), (2, 3), (3, 1), (3, 2), (3, 3),
)


class Gather:
    def __init__(self, own, buf, first, pos, core, send, recv, sib_send, sib_recv):
        self.own, self.buf, self.first, self.pos, self.core = own, buf, first, pos, core
        self.send, self.recv, self.sib_send, self.sib_recv = send, recv, sib_send, sib_recv
        self.started = []

    def place(self, second_role, first_role):
        first = lax.rem(self.pos[self.first] + OFFSETS[first_role], 4)
        other = "y" if self.first == "x" else "x"
        second = lax.rem(self.pos[other] + OFFSETS[second_role], 4)
        return (first, second) if self.first == "x" else (second, first)

    def rows(self, x, y, core):
        return pl.ds(pl.multiple_of((y * NF + x * 2 + core) * ROWS, 16), ROWS)

    def target(self, ring, step):
        axis = self.first if ring == 0 else ("y" if self.first == "x" else "x")
        index = lax.rem(self.pos[axis] + step, 4)
        return {"fsdp": index * 2 + self.core} if axis == "x" else {"dp": index}

    def part(self, roles, half):
        x, y = self.place(*roles)
        rows = self.rows(x, y, self.core)
        if half is None:
            return self.buf.at[rows, :]
        return self.buf.at[rows, pl.ds(half * HALF, HALF)]

    def copy(self, roles, half, ring, step, send_index, there):
        dst = self.part(roles, half)
        src = self.own if roles == (0, 0) else dst
        copy = pltpu.make_async_remote_copy(
            src_ref=src,
            dst_ref=dst,
            send_sem=self.send.at[send_index],
            recv_sem=self.recv.at[there],
            device_id=self.target(ring, step),
            device_id_type=MESH,
        )
        copy.start()
        self.started.append(copy)

    def to_sibling(self, roles):
        dst = self.part(roles, None)
        src = self.own if roles == (0, 0) else dst
        index = roles[0] * 4 + roles[1]
        copy = pltpu.make_async_remote_copy(
            src_ref=src,
            dst_ref=dst,
            send_sem=self.sib_send.at[index],
            recv_sem=self.sib_recv.at[index],
            device_id={"fsdp": self.pos["x"] * 2 + (1 - self.core)},
            device_id_type=MESH,
        )
        copy.start()
        self.started.append(copy)

    def ready(self, roles):
        second, first = roles
        if second == 0:
            if first == 0:
                self.copy(roles, None, 0, 1, 0, 2 * 1)
                self.copy(roles, None, 0, 3, 1, 2 * 2)
            elif first == 1:
                self.copy(roles, 0, 0, 1, 2, 2 * 3)
            elif first == 2:
                self.copy(roles, 1, 0, 3, 3, 2 * 3 + 1)
            base = 4 + 4 * first
            self.copy(roles, None, 1, 1, base, 2 * (4 * 1 + first))
            self.copy(roles, None, 1, 3, base + 1, 2 * (4 * 2 + first))
        elif second == 1:
            self.copy(roles, 0, 1, 1, 4 + 4 * first + 2, 2 * (4 * 3 + first))
        elif second == 2:
            self.copy(roles, 1, 1, 3, 4 + 4 * first + 3, 2 * (4 * 3 + first) + 1)
        self.to_sibling(roles)

    def arrive(self, roles):
        halves = (0, 1) if 3 in roles and (roles[0] == 3 or roles == (0, 3)) else (None,)
        for half in halves:
            ref = self.part(roles, half)
            pltpu.make_async_remote_copy(
                src_ref=ref,
                dst_ref=ref,
                send_sem=self.send.at[0],
                recv_sem=self.recv.at[2 * (4 * roles[0] + roles[1]) + (half or 0)],
                device_id=self.target(0, 1),
                device_id_type=MESH,
            ).wait_recv()

    def from_sibling(self, roles):
        x, y = self.place(*roles)
        ref = self.buf.at[self.rows(x, y, 1 - self.core), :]
        index = roles[0] * 4 + roles[1]
        pltpu.make_async_remote_copy(
            src_ref=ref,
            dst_ref=ref,
            send_sem=self.sib_send.at[index],
            recv_sem=self.sib_recv.at[index],
            device_id={"fsdp": self.pos["x"] * 2 + (1 - self.core)},
            device_id_type=MESH,
        ).wait_recv()


def distance_of(k):
    m = 8 - (k + 1) // 2
    return jnp.where(lax.rem(k, 2) == 1, m, LANGS - m)


def exchange(buf, axis, count, me, send, recv):
    copies = []
    for r in range(1, count):
        copy = pltpu.make_async_remote_copy(
            src_ref=buf.at[me],
            dst_ref=buf.at[me],
            send_sem=send.at[r],
            recv_sem=recv.at[r],
            device_id={axis: lax.rem(me + r, count)},
            device_id_type=MESH,
        )
        copy.start()
        copies.append(copy)
    for r in range(1, count):
        ref = buf.at[lax.rem(me + count - r, count)]
        pltpu.make_async_remote_copy(
            src_ref=ref,
            dst_ref=ref,
            send_sem=send.at[r],
            recv_sem=recv.at[r],
            device_id={axis: lax.rem(me + r, count)},
            device_id_type=MESH,
        ).wait_recv()
    return copies


def vaccinate(gram, targets, accept):
    rows = lax.broadcasted_iota(jnp.int32, (LANGS, LANGS), 0)
    cols = lax.broadcasted_iota(jnp.int32, (LANGS, LANGS), 1)
    identity = (rows == cols).astype(jnp.float32)
    allowed = accept.astype(jnp.float32) * (1.0 - identity)
    diag_col = jnp.sum(gram * identity, axis=1, keepdims=True)
    diag_row = jnp.sum(gram * identity, axis=0, keepdims=True)
    cos_pairs = gram / jnp.sqrt(diag_col * diag_row)
    roots = jnp.sqrt(1.0 - targets * targets)
    coeffs, product = identity, gram
    for j in range(LANGS):
        inner = product[:, j : j + 1]
        norm_sq = jnp.sum(product * coeffs, axis=1, keepdims=True)
        own = gram[j : j + 1, j : j + 1]
        cosine = inner / jnp.sqrt(norm_sq * own)
        root = roots[:, j : j + 1]
        sine = jnp.sqrt(jnp.maximum(1.0 - cosine * cosine, 0.0))
        step = (
            jnp.sqrt(norm_sq) * (targets[:, j : j + 1] * sine - cosine * root) / (jnp.sqrt(own) * root)
        )
        step = jnp.where(allowed[:, j : j + 1] > 0.5, step, 0.0)
        coeffs = coeffs + step * identity[j : j + 1, :]
        product = product + step * gram[j : j + 1, :]
    weights_row = jnp.sum(coeffs, axis=0, keepdims=True)
    weights_col = jnp.sum(identity * weights_row, axis=1, keepdims=True)
    quad = jnp.sum(weights_col * gram * weights_row, axis=(0, 1), keepdims=True)
    mean_square = jnp.maximum(quad, 0.0) / (2.0 * D * FF)
    factor = jnp.minimum(1.0, clip_level / jnp.sqrt(mean_square + 1e-06))
    new_targets = (1.0 - ema_rate) * targets + ema_rate * cos_pairs
    return weights_col * factor, new_targets


def kernel(
    tok_ref, cot_ref, len_ref, wup_hbm, wdn_hbm, tgt_ref, acc_ref,
    up_out, dn_out, nt_out,
    x_buf, c_buf, wup, wdn, wdn_t, p_t, h_t, outbox, inbox, pairs, st1, st2, st3, wv, comb,
    local_sem,
    t_send, t_recv, t_sib_send, t_sib_recv,
    c_send, c_recv, c_sib_send, c_sib_recv,
    a_send, a_recv, s1_send, s1_recv, s2_send, s2_recv, s3_send, s3_recv,
):
    z, y, f = lax.axis_index("lang"), lax.axis_index("dp"), lax.axis_index("fsdp")
    x, core = f // 2, lax.rem(f, 2)

    barrier = pltpu.get_barrier_semaphore()
    for axis, count, me in (("fsdp", NF, f), ("dp", NY, y), ("lang", LANGS, z)):
        for r in range(1, count):
            pl.semaphore_signal(
                barrier, inc=1, device_id={axis: lax.rem(me + r, count)}, device_id_type=MESH
            )

    pos = {"x": x, "y": y}
    tok, cot = tok_ref.at[0], cot_ref.at[0]
    tokens = Gather(tok, x_buf, "x", pos, core, t_send, t_recv, t_sib_send, t_sib_recv)
    upstream = Gather(cot, c_buf, "y", pos, core, c_send, c_recv, c_sib_send, c_sib_recv)
    mine = tokens.rows(x, y, core)
    local = [
        pltpu.make_async_copy(wdn_hbm, wdn, local_sem.at[0]),
        pltpu.make_async_copy(wup_hbm, wup, local_sem.at[1]),
        pltpu.make_async_copy(tok, x_buf.at[mine, :], local_sem.at[2]),
        pltpu.make_async_copy(cot, c_buf.at[mine, :], local_sem.at[3]),
    ]
    for copy in local:
        copy.start()

    pl.semaphore_wait(barrier, (NF - 1) + (NY - 1) + (LANGS - 1))
    tokens.ready((0, 0))
    upstream.ready((0, 0))

    for copy in local:
        copy.wait()

    @pl.loop(0, D // 256)
    def _(i):
        part = pl.ds(pl.multiple_of(i * 256, 256), 256)
        wdn_t[part, :] = wdn[:, part].T

    for roles in ARRIVALS:
        for gather in (tokens, upstream):
            gather.arrive(roles)
            gather.ready(roles)
    for roles in ((0, 0),) + ARRIVALS:
        for gather in (tokens, upstream):
            gather.from_sibling(roles)

    @pl.loop(0, LTOK // 256)
    def _(b):
        part = pl.ds(pl.multiple_of(b * 256, 256), 256)
        v = jnp.dot(x_buf[part, :], wup[...], preferred_element_type=jnp.float32)
        hg = jnp.dot(c_buf[part, :], wdn_t[...], preferred_element_type=jnp.float32)
        row = lax.broadcasted_iota(jnp.int32, (256, HID), 0)
        first, second = len_ref[0, 2 * b], len_ref[0, 2 * b + 1]
        keep = row < jnp.where(row < SEQ, first, second + SEQ)
        k = 0.7978845608028654
        sq = v * v
        t = jnp.tanh(k * (v + 0.044715 * (sq * v)))
        cdf = 0.5 * (1.0 + t)
        slope = cdf + 0.5 * v * (1.0 - t * t) * (k * (1.0 + 3.0 * 0.044715 * sq))
        p = jnp.where(keep, hg * slope, 0.0).astype(jnp.bfloat16)
        h = jnp.where(keep, v * cdf, 0.0).astype(jnp.bfloat16)
        p_t[:, part] = p.T
        h_t[:, part] = h.T

    def chunk(owner):
        part = pl.ds(pl.multiple_of(owner * DS, DS), DS)
        up = jnp.dot(p_t[...], x_buf[:, part], preferred_element_type=jnp.float32)
        dn = jnp.dot(h_t[...], c_buf[:, part], preferred_element_type=jnp.float32)
        return up.astype(jnp.bfloat16), dn.astype(jnp.bfloat16)

    def grad_copy(k, block):
        return pltpu.make_async_remote_copy(
            src_ref=outbox.at[k],
            dst_ref=inbox.at[block],
            send_sem=a_send.at[k],
            recv_sem=a_recv.at[k],
            device_id={"lang": lax.rem(z + distance_of(k), LANGS)},
            device_id_type=MESH,
        )

    @pl.loop(0, LANGS - 1)
    def _(k):
        up, dn = chunk(lax.rem(z + distance_of(k), LANGS))
        outbox[k, :, :DS] = up
        outbox[k, :, DS:] = dn
        grad_copy(k, z).start()

    up, dn = chunk(z)
    inbox[z, :, :DS] = up
    inbox[z, :, DS:] = dn

    for copy in tokens.started + upstream.started:
        copy.wait_send()

    @pl.loop(0, LANGS - 1)
    def _(k):
        grad_copy(k, lax.rem(z + LANGS - distance_of(k), LANGS)).wait_recv()

    pairs[...] = jnp.zeros_like(pairs)

    @pl.loop(0, 4)
    def _(g):
        parts = [
            inbox[:, pl.ds(pl.multiple_of(g * 64 + i * 16, 16), 16), :].reshape(256, 256)
            for i in range(4)
        ]
        a = jnp.concatenate(parts, axis=1)
        pairs[...] += lax.dot_general(
            a, a, (((1,), (1,)), ((), ())), preferred_element_type=jnp.float32
        )

    ri = lax.broadcasted_iota(jnp.int32, (256, 256), 0)
    ci = lax.broadcasted_iota(jnp.int32, (256, 256), 1)
    same = jnp.where(lax.rem(ri, 16) == lax.rem(ci, 16), pairs[...], 0.0)
    by_row = jnp.sum(same.reshape(LANGS, 16, 256), axis=1)
    li = lax.broadcasted_iota(jnp.int32, (256, 128), 0) // 16
    lj = lax.broadcasted_iota(jnp.int32, (256, 128), 1)
    select = (li == lj).astype(jnp.float32)
    st1[f] = jnp.dot(
        by_row, select, precision=lax.Precision.HIGHEST, preferred_element_type=jnp.float32
    )
    sends = exchange(st1, "fsdp", NF, f, s1_send, s1_recv)
    st2[y] = jnp.sum(st1[...], axis=0)
    sends += exchange(st2, "dp", NY, y, s2_send, s2_recv)
    st3[z] = jnp.sum(st2[...], axis=0)
    sends += exchange(st3, "lang", LANGS, z, s3_send, s3_recv)
    gram = jnp.sum(st3[...], axis=0)[:, :LANGS]

    weights, new_targets = vaccinate(gram, tgt_ref[...], acc_ref[...])
    nt_out[...] = new_targets
    wv[...] = jnp.broadcast_to(weights, (LANGS, 256))

    @pl.loop(0, 8)
    def _(r):
        rows = pl.ds(pl.multiple_of(r * 32, 32), 32)
        total = jnp.zeros((32, 256), jnp.float32)
        for l in range(LANGS):
            total = total + wv[l : l + 1, :] * inbox[l, rows, :].astype(jnp.float32)
        comb[rows, :] = total

    up_out[...] = comb[:, :DS].T
    dn_out[...] = comb[:, DS:]

    for copy in sends:
        copy.wait_send()

    @pl.loop(0, LANGS - 1)
    def _(k):
        grad_copy(k, z).wait_send()


def on_device(tokens, cotangent, lengths, up_weight, down_weight, targets, accept):
    bf16, f32 = jnp.bfloat16, jnp.float32
    dma = pltpu.SemaphoreType.DMA
    any_space = pl.BlockSpec(memory_space=pl.ANY)
    vmem = pl.BlockSpec(memory_space=pltpu.VMEM)
    return pl.pallas_call(
        kernel,
        out_shape=(
            jax.ShapeDtypeStruct((DS, HID), f32),
            jax.ShapeDtypeStruct((HID, DS), f32),
            jax.ShapeDtypeStruct((LANGS, LANGS), f32),
        ),
        in_specs=[
            any_space, any_space, pl.BlockSpec(memory_space=pltpu.SMEM), any_space, any_space, vmem, vmem,
        ],
        out_specs=(vmem, vmem, vmem),
        scratch_shapes=[
            pltpu.VMEM((LTOK, D), bf16),
            pltpu.VMEM((LTOK, D), bf16),
            pltpu.VMEM((D, HID), bf16),
            pltpu.VMEM((HID, D), bf16),
            pltpu.VMEM((D, HID), bf16),
            pltpu.VMEM((HID, LTOK), bf16),
            pltpu.VMEM((HID, LTOK), bf16),
            pltpu.VMEM((LANGS - 1, HID, 2 * DS), bf16),
            pltpu.VMEM((LANGS, HID, 2 * DS), bf16),
            pltpu.VMEM((256, 256), f32),
            pltpu.VMEM((NF, LANGS, 128), f32),
            pltpu.VMEM((NY, LANGS, 128), f32),
            pltpu.VMEM((LANGS, LANGS, 128), f32),
            pltpu.VMEM((LANGS, 256), f32),
            pltpu.VMEM((HID, 2 * DS), f32),
            dma((4,)),
            dma((20,)), dma((32,)), dma((16,)), dma((16,)),
            dma((20,)), dma((32,)), dma((16,)), dma((16,)),
            dma((LANGS - 1,)), dma((LANGS - 1,)),
            dma((NF,)), dma((NF,)), dma((NY,)), dma((NY,)), dma((LANGS,)), dma((LANGS,)),
        ],
        compiler_params=pltpu.CompilerParams(
            collective_id=0, has_side_effects=True, vmem_limit_bytes=48 * 1024 * 1024
        ),
        cost_estimate=pl.CostEstimate(
            flops=4 * 2 * LTOK * D * HID, bytes_accessed=4 * 1024 * 1024, transcendentals=LTOK * HID
        ),
        name="vaccine_step",
    )(tokens, cotangent, lengths, up_weight, down_weight, targets, accept)


def solution(mesh):
    in_specs = (
        P("lang", ("dp", "fsdp"), None),
        P("lang", ("dp", "fsdp"), None),
        P("lang", None),
        P(None, ("dp", "fsdp")),
        P(("dp", "fsdp"), None),
        P(),
        P(),
    )
    out_specs = (P("lang", ("dp", "fsdp")), P(("dp", "fsdp"), "lang"), P())
    return jax.shard_map(
        on_device, mesh=mesh, in_specs=in_specs, out_specs=out_specs, check_vma=False
    )
```

time: 572 us -> 185 us (0.32)
  blocking collectives: 207 us -> 0 us
  waiting for transfers between devices: 188 us -> 0 us
  Pallas kernels: 0 us -> 173 us
  matrix products: 58.7 us -> 0 us
  local copies, waits for them, and re-layouts: 37.8 us -> 8.25 us
  other arithmetic: 27.7 us -> 0 us
  starting transfers between devices: 24.5 us -> 0 us
  between operations: 16.2 us -> 0.66 us
  loops' own time: 11.3 us -> 0 us
    psum x2 -> x0, blocking collectives: 207 us -> none  [the longest x1 109 us: on_device(): gram_sums = lax.psum(partial_value, ('lang', 'dp', 'fsdp'))]
    pallas_call x0 -> x1, Pallas kernels: none -> 173 us  [on_device(): pl.pallas_call(kernel, out_shape=(jax.ShapeDtypeStruct((DS, HID), f32), j...]
    all_gather x2 -> x0, waiting for transfers between devices: 134 us -> none  [the longest x1 71.9 us: on_device(): lax.all_gather(tokens, ('dp', 'fsdp'), axis=1, tiled=True)]
    dot_general x103 -> x0, matrix products: 58.7 us -> none  [the longest x1 12.9 us: token_grads(): lax.dot_general(inputs, preact_grad, (((0,), (0,)), ((), ())), preferred_...]
    all_to_all x2 -> x0, waiting for transfers between devices: 52.8 us -> none  [the longest x1 37.6 us: on_device(): lax.all_to_all(outgoing[1], 'lang', split_axis=1, concat_axis=0, tiled=True)]
    all_to_all x2 -> x0, starting transfers between devices: 24.4 us -> none  [the longest x1 12.2 us: on_device(): lax.all_to_all(outgoing[0], 'lang', split_axis=1, concat_axis=0, tiled=True)]
    unnamed x2 -> x0, other arithmetic: 23.2 us -> none
    broadcast_in_dim x2 -> x0, local copies, waits for them, and re-layouts: 16.3 us -> none  [the longest x1 11.7 us: on_device(): g_dt.astype(jnp.bfloat16)[None]]
  transfers between devices with their start and end apart: 4 -> 0, of which waited for: 4 -> 0; matrix products, arithmetic and copies ran while one was open for 8% -> 0% of each run, Pallas kernels for 0% -> 0%
where the time goes in v1:
time: 185 us; the launch traced here: 182 us
  Pallas kernels  173 us (94%)
  local copies, waits for them, and re-layouts  8.25 us (4%)
    pallas_call x1, Pallas kernels, on_device(): pl.pallas_call(kernel, out_shape=(jax.ShapeDtypeStruct((DS, HID), f32), j...  173 us
    unnamed x17, local copies, waits for them, and re-layouts  8.25 us

profile of v1, /device:TPU:1, one launch (start us, length us, event | category | flops | bytes accessed | tf_op | source)
XLA Modules:
  0.0 181.6 jit_solution(2944154064074081826)
XLA Ops:
  0.6 0.0 copy-start
  0.6 1.2 copy-done
  1.9 0.0 copy-start.1
  1.9 1.2 copy-done.1
  3.1 0.0 copy-start.2
  3.1 0.9 copy-done.2
  4.0 0.0 copy-start.3
  4.0 0.9 copy-done.3
  4.9 0.0 copy-start.4
  4.9 0.7 copy-done.4
  5.6 0.0 copy-start.5
  5.6 0.7 copy-done.5
  6.3 0.0 copy-start.6
  6.3 0.7 copy-done.6
  7.0 172.7 %vaccine_step.1 = (f32[128,256]{1,0:T(8,128)S(1)}, f32[256,128]{1,0:T(8,128)S(1)}, f32[16,16]{1,0:T(8,128)S(1)}) custom-call(bf16[1,48,2048]{2,1,0:T(8,128)(2,1)S(1)} %copy-done.2, bf16[1,48,2048]{2,1,0:T(8,128)(2,1)S(1)} %copy-done.3, s32[1,12]{1,0:T(1,128)S(1)} %copy-done.6, bf16[2048,256]{1,0:T(8,128)(2,1)S(1)} %copy-done, ...), custom_call_target="tpu_custom_call" | custom-call | flops 6442450944 | bytes 4194304 | tf_op jit(solution)/shard_map/vaccine_step/pallas_call | solution.py:362
  179.7 0.7 copy.13
  180.4 0.7 copy.14
  181.0 0.6 copy.15
Async XLA Ops:
  0.6 1.2 copy-start
  1.9 1.2 copy-start.1
  3.1 0.9 copy-start.2
  4.0 0.9 copy-start.3
  4.9 0.7 copy-start.4
  5.6 0.7 copy-start.5
  6.3 0.7 copy-start.6

commit v2 on v1

v2 whole, which is shorter than its diff:
```python
import functools

import jax
import jax.numpy as jnp
from jax import lax
from jax.experimental import pallas as pl
from jax.experimental.pallas import tpu as pltpu
from jax.sharding import PartitionSpec as P

D = 2048
FF = 8192
SEQ = 128
LTOK = 1536
LANGS = 16
NY = 4
NX = 4
NF = 8
ROWS = 48
HID = 256
DS = 128
HALF = D // 2

ema_rate = 0.01
clip_level = 0.25
MESH = pl.DeviceIdType.MESH

OFFSETS = (0, 3, 1, 2)
ARRIVALS = (
    (0, 1), (0, 2), (1, 0), (2, 0), (0, 3), (1, 1), (2, 1), (1, 2), (2, 2),
    (1, 3), (2, 3), (3, 0), (3, 1), (3, 2), (3, 3),
)
EARLY = 4


class Plane:
    def __init__(self, x, y, core):
        self.x, self.y, self.core = x, y, core
        self.next = {}
        for ring in (0, 1):
            for step in (1, 3):
                dx = jnp.where(core == ring, step, 0)
                self.next[ring, step] = {
                    "dp": lax.rem(y + step - dx, 4),
                    "fsdp": lax.rem(x + dx, 4) * 2 + core,
                }
        self.sibling = {"fsdp": x * 2 + (1 - core)}

    def first_token(self, which, second, first):
        core = self.core if which == 0 else 1 - self.core
        dx = jnp.where(core == 0, OFFSETS[first], OFFSETS[second])
        dy = OFFSETS[first] + OFFSETS[second] - dx
        return (lax.rem(self.y + dy, 4) * NF + lax.rem(self.x + dx, 4) * 2 + core) * ROWS


class Gather:
    def __init__(self, plane, own, buf, start, width, send, recv, sib_send, sib_recv):
        self.plane, self.own, self.buf, self.start, self.width = plane, own, buf, start, width
        self.send, self.recv, self.sib_send, self.sib_recv = send, recv, sib_send, sib_recv
        self.started = []

    def part(self, roles, half):
        if half is None:
            return self.buf.at[0, roles[0], roles[1], :, pl.ds(self.start, self.width)]
        width = self.width // 2
        return self.buf.at[0, roles[0], roles[1], :, pl.ds(self.start + half * width, width)]

    def copy(self, roles, half, ring, step, send_index, there):
        src = self.own if roles == (0, 0) else self.part(roles, half)
        copy = pltpu.make_async_remote_copy(
            src_ref=src,
            dst_ref=self.part(there, half),
            send_sem=self.send.at[send_index],
            recv_sem=self.recv.at[2 * (4 * there[0] + there[1]) + (half or 0)],
            device_id=self.plane.next[ring, step],
            device_id_type=MESH,
        )
        copy.start()
        self.started.append(copy)

    def sibling_copy(self, second):
        cols = pl.ds(self.start, self.width)
        return pltpu.make_async_remote_copy(
            src_ref=self.buf.at[0, second, :, :, cols],
            dst_ref=self.buf.at[1, second, :, :, cols],
            send_sem=self.sib_send.at[second],
            recv_sem=self.sib_recv.at[second],
            device_id=self.plane.sibling,
            device_id_type=MESH,
        )

    def to_sibling(self, second):
        copy = self.sibling_copy(second)
        copy.start()
        self.started.append(copy)

    def from_sibling(self, second):
        self.sibling_copy(second).wait_recv()

    def ready(self, roles):
        second, first = roles
        base = 4 + 4 * first
        if second == 0:
            if first == 0:
                self.copy(roles, None, 0, 1, 0, (0, 1))
                self.copy(roles, None, 0, 3, 1, (0, 2))
            elif first == 1:
                self.copy(roles, 0, 0, 1, 2, (0, 3))
            elif first == 2:
                self.copy(roles, 1, 0, 3, 3, (0, 3))
            self.copy(roles, None, 1, 1, base, (1, first))
            self.copy(roles, None, 1, 3, base + 1, (2, first))
        elif second == 1:
            self.copy(roles, 0, 1, 1, base + 2, (3, first))
        elif second == 2:
            self.copy(roles, 1, 1, 3, base + 3, (3, first))

    def arrive(self, roles):
        for half in (0, 1) if roles[0] == 3 or roles == (0, 3) else (None,):
            ref = self.part(roles, half)
            pltpu.make_async_remote_copy(
                src_ref=ref,
                dst_ref=ref,
                send_sem=self.send.at[0],
                recv_sem=self.recv.at[2 * (4 * roles[0] + roles[1]) + (half or 0)],
                device_id=self.plane.next[0, 1],
                device_id_type=MESH,
            ).wait_recv()

    def step(self, roles):
        self.arrive(roles)
        self.ready(roles)
        if roles in ((0, 3), (1, 3), (2, 3), (3, 3)):
            self.to_sibling(roles[0])


def distance_of(k):
    m = 8 - (k + 1) // 2
    return jnp.where(lax.rem(k, 2) == 1, m, LANGS - m)


def exchange(buf, axis, count, me, send, recv):
    copies = []
    for r in range(1, count):
        copy = pltpu.make_async_remote_copy(
            src_ref=buf.at[me],
            dst_ref=buf.at[me],
            send_sem=send.at[r],
            recv_sem=recv.at[r],
            device_id={axis: lax.rem(me + r, count)},
            device_id_type=MESH,
        )
        copy.start()
        copies.append(copy)
    for r in range(1, count):
        ref = buf.at[lax.rem(me + count - r, count)]
        pltpu.make_async_remote_copy(
            src_ref=ref,
            dst_ref=ref,
            send_sem=send.at[r],
            recv_sem=recv.at[r],
            device_id={axis: lax.rem(me + r, count)},
            device_id_type=MESH,
        ).wait_recv()
    return copies


def vaccinate(gram, targets, accept):
    rows = lax.broadcasted_iota(jnp.int32, (LANGS, LANGS), 0)
    cols = lax.broadcasted_iota(jnp.int32, (LANGS, LANGS), 1)
    identity = (rows == cols).astype(jnp.float32)
    allowed = accept.astype(jnp.float32) * (1.0 - identity)
    diag_col = jnp.sum(gram * identity, axis=1, keepdims=True)
    diag_row = jnp.sum(gram * identity, axis=0, keepdims=True)
    cos_pairs = gram / jnp.sqrt(diag_col * diag_row)
    roots = jnp.sqrt(1.0 - targets * targets)
    coeffs, product = identity, gram
    for j in range(LANGS):
        inner = product[:, j : j + 1]
        norm_sq = jnp.sum(product * coeffs, axis=1, keepdims=True)
        own = gram[j : j + 1, j : j + 1]
        cosine = inner / jnp.sqrt(norm_sq * own)
        root = roots[:, j : j + 1]
        sine = jnp.sqrt(jnp.maximum(1.0 - cosine * cosine, 0.0))
        step = (
            jnp.sqrt(norm_sq) * (targets[:, j : j + 1] * sine - cosine * root) / (jnp.sqrt(own) * root)
        )
        step = jnp.where(allowed[:, j : j + 1] > 0.5, step, 0.0)
        coeffs = coeffs + step * identity[j : j + 1, :]
        product = product + step * gram[j : j + 1, :]
    weights_row = jnp.sum(coeffs, axis=0, keepdims=True)
    weights_col = jnp.sum(identity * weights_row, axis=1, keepdims=True)
    quad = jnp.sum(weights_col * gram * weights_row, axis=(0, 1), keepdims=True)
    mean_square = jnp.maximum(quad, 0.0) / (2.0 * D * FF)
    factor = jnp.minimum(1.0, clip_level / jnp.sqrt(mean_square + 1e-06))
    new_targets = (1.0 - ema_rate) * targets + ema_rate * cos_pairs
    return weights_col * factor, new_targets


def kernel(
    tok_ref, cot_ref, len_hbm, wup_hbm, wdn_hbm, tgt_hbm, acc_hbm,
    up_out, dn_out, nt_out,
    x_buf, c_buf, wup, wdn, wdn_t, tgt, acc, lens, v_buf, hp, h_t, p_t,
    out_dn, out_up, in_dn, in_up, pairs, st1, st2, st3, wv, comb,
    local_sem, cols_sem,
    t_send, t_recv, t_sib_send, t_sib_recv,
    e_send, e_recv, e_sib_send, e_sib_recv,
    l_send, l_recv, l_sib_send, l_sib_recv,
    d_send, d_recv, u_send, u_recv, s1_send, s1_recv, s2_send, s2_recv, s3_send, s3_recv,
):
    z, y, f = lax.axis_index("lang"), lax.axis_index("dp"), lax.axis_index("fsdp")
    x, core = f // 2, lax.rem(f, 2)

    barrier = pltpu.get_barrier_semaphore()
    for axis, count, me in (("fsdp", NF, f), ("dp", NY, y), ("lang", LANGS, z)):
        for r in range(1, count):
            pl.semaphore_signal(
                barrier, inc=1, device_id={axis: lax.rem(me + r, count)}, device_id_type=MESH
            )

    def owner(k):
        return lax.rem(z + (distance_of(k) if not isinstance(k, int) or k < 15 else 0), LANGS)

    def columns(block):
        return pl.ds(pl.multiple_of(block * DS, DS), DS)

    plane = Plane(x, y, core)
    tok, cot = tok_ref.at[0], cot_ref.at[0]
    cot_copies = [
        pltpu.make_async_copy(
            cot.at[:, columns(owner(k))], c_buf.at[0, 0, 0, :, pl.ds(k * DS, DS)], cols_sem.at[k]
        )
        for k in range(LANGS)
    ]
    local = [
        pltpu.make_async_copy(tok, x_buf.at[0, 0, 0], local_sem.at[0]),
        pltpu.make_async_copy(wdn_hbm, wdn, local_sem.at[1]),
        pltpu.make_async_copy(wup_hbm, wup, local_sem.at[2]),
        pltpu.make_async_copy(tgt_hbm, tgt, local_sem.at[3]),
        pltpu.make_async_copy(acc_hbm, acc, local_sem.at[4]),
        pltpu.make_async_copy(len_hbm, lens, local_sem.at[5]),
    ]
    for copy in cot_copies + local:
        copy.start()

    early = EARLY * DS
    tokens = Gather(plane, tok, x_buf, 0, D, t_send, t_recv, t_sib_send, t_sib_recv)
    first = Gather(
        plane, c_buf.at[0, 0, 0, :, pl.ds(0, early)], c_buf, 0, early,
        e_send, e_recv, e_sib_send, e_sib_recv,
    )
    rest = Gather(
        plane, c_buf.at[0, 0, 0, :, pl.ds(early, D - early)], c_buf, early, D - early,
        l_send, l_recv, l_sib_send, l_sib_recv,
    )

    pl.semaphore_wait(barrier, (NF - 1) + (NY - 1) + (LANGS - 1))
    tokens.ready((0, 0))
    for copy in cot_copies:
        copy.wait()
    first.ready((0, 0))
    for copy in local:
        copy.wait()

    for k in range(LANGS):
        wdn_t[pl.ds(k * DS, DS), :] = wdn[:, columns(owner(k))].T

    def activate(which, second):
        base = (which * 4 + second) * 192
        v_buf[pl.ds(base, 192), :] = jnp.dot(
            x_buf[which, second].reshape(192, D), wup[...], preferred_element_type=jnp.float32
        )
        for i in range(4):
            token = plane.first_token(which, second, i)
            slot = token // SEQ
            offset = token - slot * SEQ
            here, after = lens[0, slot], lens[0, jnp.minimum(slot + 1, 11)]
            place = lax.broadcasted_iota(jnp.int32, (ROWS, HID), 0) + offset
            keep = place < jnp.where(place < SEQ, here, after + SEQ)
            rows = pl.ds(base + i * ROWS, ROWS)
            v = v_buf[rows, :]
            k = 0.7978845608028654
            sq = v * v
            t = jnp.tanh(k * (v + 0.044715 * (sq * v)))
            cdf = 0.5 * (1.0 + t)
            slope = cdf + 0.5 * v * (1.0 - t * t) * (k * (1.0 + 3.0 * 0.044715 * sq))
            hp[rows, :] = jnp.where(keep, v * cdf, 0.0).astype(jnp.bfloat16)
            v_buf[rows, :] = jnp.where(keep, slope, 0.0)

    def turn(dst, start, count):
        for i in range(start, start + count):
            dst[:, pl.ds(i * 128, 128)] = hp[pl.ds(i * 128, 128), :].T

    for n, roles in enumerate(ARRIVALS):
        tokens.step(roles)
        first.step(roles)
        if roles == (2, 1):
            tokens.from_sibling(0)
            activate(0, 0)
            rest.ready((0, 0))
        elif roles == (2, 2):
            activate(1, 0)
        elif roles == (2, 3):
            activate(0, 1)
        elif roles == (3, 0):
            tokens.from_sibling(1)
            activate(1, 1)
        elif roles == (3, 1):
            activate(0, 2)
        elif roles == (3, 2):
            tokens.from_sibling(2)
            activate(1, 2)
    turn(h_t, 0, 3)
    turn(h_t, 6, 3)
    activate(0, 3)
    tokens.from_sibling(3)
    activate(1, 3)
    turn(h_t, 3, 3)
    turn(h_t, 9, 3)
    for second in range(4):
        first.from_sibling(second)

    def down(k):
        return jnp.dot(
            h_t[...],
            c_buf[:, :, :, :, columns(k)].reshape(LTOK, DS),
            preferred_element_type=jnp.float32,
        ).astype(jnp.bfloat16)

    def grad_copy(out, inbox, k, block, send, recv):
        return pltpu.make_async_remote_copy(
            src_ref=out.at[k],
            dst_ref=inbox.at[block],
            send_sem=send.at[k],
            recv_sem=recv.at[k],
            device_id={"lang": owner(k)},
            device_id_type=MESH,
        )

    @pl.loop(0, EARLY)
    def _(k):
        out_dn[k] = down(k)
        grad_copy(out_dn, in_dn, k, z, d_send, d_recv).start()

    for roles in ARRIVALS:
        rest.step(roles)
    for second in range(4):
        rest.from_sibling(second)

    @pl.loop(EARLY, LANGS - 1)
    def _(k):
        out_dn[k] = down(k)
        grad_copy(out_dn, in_dn, k, z, d_send, d_recv).start()

    in_dn[z] = down(LANGS - 1)

    for group in range(8):
        hg = jnp.dot(
            c_buf[group // 4, group % 4].reshape(192, D), wdn_t[...], preferred_element_type=jnp.float32
        )
        rows = pl.ds(group * 192, 192)
        hp[rows, :] = (hg * v_buf[rows, :]).astype(jnp.bfloat16)
    turn(p_t, 0, 12)

    def up(block):
        return jnp.dot(
            p_t[...],
            x_buf[:, :, :, :, columns(block)].reshape(LTOK, DS),
            preferred_element_type=jnp.float32,
        ).astype(jnp.bfloat16)

    @pl.loop(0, LANGS - 1)
    def _(k):
        out_up[k] = up(owner(k))
        grad_copy(out_up, in_up, k, z, u_send, u_recv).start()

    in_up[z] = up(z)

    for copy in tokens.started + first.started + rest.started:
        copy.wait_send()

    pairs[...] = jnp.zeros_like(pairs)

    for inbox, out, send, recv in ((in_dn, out_dn, d_send, d_recv), (in_up, out_up, u_send, u_recv)):

        @pl.loop(0, LANGS - 1)
        def _(k):
            source = lax.rem(z + LANGS - distance_of(k), LANGS)
            grad_copy(out, inbox, k, source, send, recv).wait_recv()

        @pl.loop(0, 2)
        def _(g):
            a = jnp.concatenate(
                [
                    inbox[:, pl.ds(pl.multiple_of(g * 128 + i * 16, 16), 16), :].reshape(256, DS)
                    for i in range(8)
                ],
                axis=1,
            )
            pairs[...] += lax.dot_general(
                a, a, (((1,), (1,)), ((), ())), preferred_element_type=jnp.float32
            )

    ri = lax.broadcasted_iota(jnp.int32, (256, 256), 0)
    ci = lax.broadcasted_iota(jnp.int32, (256, 256), 1)
    same = jnp.where(lax.rem(ri, 16) == lax.rem(ci, 16), pairs[...], 0.0)
    by_row = jnp.sum(same.reshape(LANGS, 16, 256), axis=1)
    li = lax.broadcasted_iota(jnp.int32, (256, 128), 0) // 16
    lj = lax.broadcasted_iota(jnp.int32, (256, 128), 1)
    select = (li == lj).astype(jnp.float32)
    st1[f] = jnp.dot(
        by_row, select, precision=lax.Precision.HIGHEST, preferred_element_type=jnp.float32
    )
    sends = exchange(st1, "fsdp", NF, f, s1_send, s1_recv)
    st2[y] = jnp.sum(st1[...], axis=0)
    sends += exchange(st2, "dp", NY, y, s2_send, s2_recv)
    st3[z] = jnp.sum(st2[...], axis=0)
    sends += exchange(st3, "lang", LANGS, z, s3_send, s3_recv)
    gram = jnp.sum(st3[...], axis=0)[:, :LANGS]

    weights, new_targets = vaccinate(gram, tgt[...], acc[...])
    nt_out[...] = new_targets
    wv[...] = jnp.broadcast_to(weights, (LANGS, DS))

    for inbox, half in ((in_up, 0), (in_dn, 1)):

        @pl.loop(0, 4)
        def _(r):
            rows = pl.ds(pl.multiple_of(r * 64, 64), 64)
            total = jnp.zeros((64, DS), jnp.float32)
            for l in range(LANGS):
                total = total + wv[l : l + 1, :] * inbox[l, rows, :].astype(jnp.float32)
            if half == 0:
                comb[rows, :] = total
            else:
                dn_out[rows, :] = total

    up_out[...] = comb[...].T

    for copy in sends:
        copy.wait_send()

    @pl.loop(0, LANGS - 1)
    def _(k):
        grad_copy(out_dn, in_dn, k, z, d_send, d_recv).wait_send()
        grad_copy(out_up, in_up, k, z, u_send, u_recv).wait_send()


def on_device(tokens, cotangent, lengths, up_weight, down_weight, targets, accept):
    bf16, f32 = jnp.bfloat16, jnp.float32
    dma = pltpu.SemaphoreType.DMA
    any_space = pl.BlockSpec(memory_space=pl.ANY)
    vmem = pl.BlockSpec(memory_space=pltpu.VMEM)
    return pl.pallas_call(
        kernel,
        out_shape=(
            jax.ShapeDtypeStruct((DS, HID), f32),
            jax.ShapeDtypeStruct((HID, DS), f32),
            jax.ShapeDtypeStruct((LANGS, LANGS), f32),
        ),
        in_specs=[any_space] * 7,
        out_specs=(vmem, vmem, vmem),
        scratch_shapes=[
            pltpu.VMEM((2, 4, 4, ROWS, D), bf16),
            pltpu.VMEM((2, 4, 4, ROWS, D), bf16),
            pltpu.VMEM((D, HID), bf16),
            pltpu.VMEM((HID, D), bf16),
            pltpu.VMEM((D, HID), bf16),
            pltpu.VMEM((LANGS, LANGS), f32),
            pltpu.VMEM((LANGS, LANGS), jnp.int32),
            pltpu.SMEM((1, 12), jnp.int32),
            pltpu.VMEM((LTOK, HID), f32),
            pltpu.VMEM((LTOK, HID), bf16),
            pltpu.VMEM((HID, LTOK), bf16),
            pltpu.VMEM((HID, LTOK), bf16),
            pltpu.VMEM((LANGS - 1, HID, DS), bf16),
            pltpu.VMEM((LANGS - 1, HID, DS), bf16),
            pltpu.VMEM((LANGS, HID, DS), bf16),
            pltpu.VMEM((LANGS, HID, DS), bf16),
            pltpu.VMEM((256, 256), f32),
            pltpu.VMEM((NF, LANGS, 128), f32),
            pltpu.VMEM((NY, LANGS, 128), f32),
            pltpu.VMEM((LANGS, LANGS, 128), f32),
            pltpu.VMEM((LANGS, DS), f32),
            pltpu.VMEM((HID, DS), f32),
            dma((6,)), dma((LANGS,)),
            dma((20,)), dma((32,)), dma((4,)), dma((4,)),
            dma((20,)), dma((32,)), dma((4,)), dma((4,)),
            dma((20,)), dma((32,)), dma((4,)), dma((4,)),
            dma((LANGS - 1,)), dma((LANGS - 1,)), dma((LANGS - 1,)), dma((LANGS - 1,)),
            dma((NF,)), dma((NF,)), dma((NY,)), dma((NY,)), dma((LANGS,)), dma((LANGS,)),
        ],
        compiler_params=pltpu.CompilerParams(
            collective_id=0, has_side_effects=True, vmem_limit_bytes=60 * 1024 * 1024
        ),
        cost_estimate=pl.CostEstimate(
            flops=4 * 2 * LTOK * D * HID, bytes_accessed=4 * 1024 * 1024, transcendentals=LTOK * HID
        ),
        name="vaccine_step",
    )(tokens, cotangent, lengths, up_weight, down_weight, targets, accept)


def solution(mesh):
    in_specs = (
        P("lang", ("dp", "fsdp"), None),
        P("lang", ("dp", "fsdp"), None),
        P("lang", None),
        P(None, ("dp", "fsdp")),
        P(("dp", "fsdp"), None),
        P(),
        P(),
    )
    out_specs = (P("lang", ("dp", "fsdp")), P(("dp", "fsdp"), "lang"), P())
    return jax.shard_map(
        on_device, mesh=mesh, in_specs=in_specs, out_specs=out_specs, check_vma=False
    )
```

time: 185 us -> 167 us (0.903); the launches traced: 182 us -> 166 us
  Pallas kernels: 173 us -> 162 us
  local copies, waits for them, and re-layouts: 8.25 us -> 2.9 us
    pallas_call x1, Pallas kernels: 173 us -> 162 us  [on_device(): pl.pallas_call(kernel, out_shape=(jax.ShapeDtypeStruct((DS, HID), f32), j...]
    unnamed x17 -> x7, local copies, waits for them, and re-layouts: 8.25 us -> 2.9 us
where the time goes in v2:
time: 167 us; the launch traced here: 166 us
  Pallas kernels  162 us (97%)
  local copies, waits for them, and re-layouts  2.9 us (2%)
    pallas_call x1, Pallas kernels, on_device(): pl.pallas_call(kernel, out_shape=(jax.ShapeDtypeStruct((DS, HID), f32), j...  162 us

profile of v2, /device:TPU:1, one launch (start us, length us, event | category | flops | bytes accessed | tf_op | source)
XLA Modules:
  0.0 165.8 jit_solution(15067010225801378037)
XLA Ops:
  0.6 162.3 %vaccine_step.1 = (f32[128,256]{1,0:T(8,128)}, f32[256,128]{1,0:T(8,128)}, f32[16,16]{1,0:T(8,128)}) custom-call(bf16[1,48,2048]{2,1,0:T(8,128)(2,1)} %tok_ref.1, bf16[1,48,2048]{2,1,0:T(8,128)(2,1)} %cot_ref.1, s32[1,12]{1,0:T(1,128)} %len_hbm.1, bf16[2048,256]{1,0:T(8,128)(2,1)} %wup_hbm.1, bf16[256,2048]{1,0:T(8,128)(2,1)} %wdn_hbm.1, f32[16,16]{1,0:T(8,128)} %tgt_hbm.1, ...), custom_call_target="tpu_custom_call" | custom-call | flops 6442450944 | bytes 4194304 | tf_op jit(solution)/shard_map/vaccine_step/pallas_call | solution.py:453
  162.9 0.0 copy-start
  162.9 1.6 copy.13
  164.5 0.0 copy-done
  164.5 0.0 copy-start.1
  164.5 0.7 copy.14
  165.2 0.0 copy-done.1
  165.2 0.6 copy.15
Async XLA Ops:
  162.9 1.6 copy-start
  164.5 0.7 copy-start.1

commit v3 on v2

--- a/solution.py
+++ b/solution.py
@@ -133,9 +133,9 @@
             self.to_sibling(roles[0])
 
 
-def distance_of(k):
+def distance_of(k, sign):
     m = 8 - (k + 1) // 2
-    return jnp.where(lax.rem(k, 2) == 1, m, LANGS - m)
+    return jnp.where(lax.rem(k, 2) == sign, LANGS - m, m)
 
 
 def exchange(buf, axis, count, me, send, recv):
@@ -164,48 +164,49 @@
     return copies
 
 
-def vaccinate(gram, targets, accept):
+def vaccinate(gram, targets_t, accept_t):
     rows = lax.broadcasted_iota(jnp.int32, (LANGS, LANGS), 0)
     cols = lax.broadcasted_iota(jnp.int32, (LANGS, LANGS), 1)
     identity = (rows == cols).astype(jnp.float32)
-    allowed = accept.astype(jnp.float32) * (1.0 - identity)
+    roots = jnp.sqrt(1.0 - targets_t * targets_t)
     diag_col = jnp.sum(gram * identity, axis=1, keepdims=True)
     diag_row = jnp.sum(gram * identity, axis=0, keepdims=True)
     cos_pairs = gram / jnp.sqrt(diag_col * diag_row)
-    roots = jnp.sqrt(1.0 - targets * targets)
+    inverse = 1.0 / jnp.sqrt(diag_col)
+    scale = inverse / roots
+    allowed = accept_t.astype(jnp.float32) * (1.0 - identity)
     coeffs, product = identity, gram
     for j in range(LANGS):
-        inner = product[:, j : j + 1]
-        norm_sq = jnp.sum(product * coeffs, axis=1, keepdims=True)
-        own = gram[j : j + 1, j : j + 1]
-        cosine = inner / jnp.sqrt(norm_sq * own)
-        root = roots[:, j : j + 1]
+        norm_sq = jnp.sum(product * coeffs, axis=0, keepdims=True)
+        over_norm = lax.rsqrt(norm_sq)
+        cosine = product[j : j + 1, :] * inverse[j : j + 1, :] * over_norm
         sine = jnp.sqrt(jnp.maximum(1.0 - cosine * cosine, 0.0))
         step = (
-            jnp.sqrt(norm_sq) * (targets[:, j : j + 1] * sine - cosine * root) / (jnp.sqrt(own) * root)
-        )
-        step = jnp.where(allowed[:, j : j + 1] > 0.5, step, 0.0)
-        coeffs = coeffs + step * identity[j : j + 1, :]
-        product = product + step * gram[j : j + 1, :]
-    weights_row = jnp.sum(coeffs, axis=0, keepdims=True)
-    weights_col = jnp.sum(identity * weights_row, axis=1, keepdims=True)
-    quad = jnp.sum(weights_col * gram * weights_row, axis=(0, 1), keepdims=True)
+            (norm_sq * over_norm)
+            * (targets_t[j : j + 1, :] * sine - cosine * roots[j : j + 1, :])
+            * scale[j : j + 1, :]
+        )
+        step = jnp.where(allowed[j : j + 1, :] > 0.5, step, 0.0)
+        coeffs = jnp.where(rows == j, coeffs + step, coeffs)
+        product = product + gram[:, j : j + 1] * step
+    weights = jnp.sum(coeffs, axis=1, keepdims=True)
+    along = jnp.sum(product, axis=1, keepdims=True)
+    quad = jnp.sum(weights * along, axis=0, keepdims=True)
     mean_square = jnp.maximum(quad, 0.0) / (2.0 * D * FF)
     factor = jnp.minimum(1.0, clip_level / jnp.sqrt(mean_square + 1e-06))
-    new_targets = (1.0 - ema_rate) * targets + ema_rate * cos_pairs
-    return weights_col * factor, new_targets
+    return weights * factor, cos_pairs
 
 
 def kernel(
     tok_ref, cot_ref, len_hbm, wup_hbm, wdn_hbm, tgt_hbm, acc_hbm,
     up_out, dn_out, nt_out,
     x_buf, c_buf, wup, wdn, wdn_t, tgt, acc, lens, v_buf, hp, h_t, p_t,
-    out_dn, out_up, in_dn, in_up, pairs, st1, st2, st3, wv, comb,
+    out_dn, out_up, in_dn, in_up, relay, pairs, st1, st2, st3, wv, comb,
     local_sem, cols_sem,
     t_send, t_recv, t_sib_send, t_sib_recv,
     e_send, e_recv, e_sib_send, e_sib_recv,
     l_send, l_recv, l_sib_send, l_sib_recv,
-    d_send, d_recv, u_send, u_recv, s1_send, s1_recv, s2_send, s2_recv, s3_send, s3_recv,
+    d_send, d_recv, u_send, u_recv, r_send, r_recv, s1_send, s1_recv, s2_send, s2_recv, s3_send, s3_recv,
 ):
     z, y, f = lax.axis_index("lang"), lax.axis_index("dp"), lax.axis_index("fsdp")
     x, core = f // 2, lax.rem(f, 2)
@@ -217,8 +218,8 @@
                 barrier, inc=1, device_id={axis: lax.rem(me + r, count)}, device_id_type=MESH
             )
 
-    def owner(k):
-        return lax.rem(z + (distance_of(k) if not isinstance(k, int) or k < 15 else 0), LANGS)
+    def owner(k, sign):
+        return lax.rem(z + (distance_of(k, sign) if not isinstance(k, int) or k < 15 else 0), LANGS)
 
     def columns(block):
         return pl.ds(pl.multiple_of(block * DS, DS), DS)
@@ -227,7 +228,7 @@
     tok, cot = tok_ref.at[0], cot_ref.at[0]
     cot_copies = [
         pltpu.make_async_copy(
-            cot.at[:, columns(owner(k))], c_buf.at[0, 0, 0, :, pl.ds(k * DS, DS)], cols_sem.at[k]
+            cot.at[:, columns(owner(k, 1))], c_buf.at[0, 0, 0, :, pl.ds(k * DS, DS)], cols_sem.at[k]
         )
         for k in range(LANGS)
     ]
@@ -262,7 +263,7 @@
         copy.wait()
 
     for k in range(LANGS):
-        wdn_t[pl.ds(k * DS, DS), :] = wdn[:, columns(owner(k))].T
+        wdn_t[pl.ds(k * DS, DS), :] = wdn[:, columns(owner(k, 1))].T
 
     def activate(which, second):
         base = (which * 4 + second) * 192
@@ -326,20 +327,33 @@
             preferred_element_type=jnp.float32,
         ).astype(jnp.bfloat16)
 
-    def grad_copy(out, inbox, k, block, send, recv):
+    def remote(src, dst, send, recv, to):
         return pltpu.make_async_remote_copy(
-            src_ref=out.at[k],
-            dst_ref=inbox.at[block],
-            send_sem=send.at[k],
-            recv_sem=recv.at[k],
-            device_id={"lang": owner(k)},
-            device_id_type=MESH,
-        )
-
-    @pl.loop(0, EARLY)
+            src_ref=src, dst_ref=dst, send_sem=send, recv_sem=recv, device_id={"lang": to}, device_id_type=MESH
+        )
+
+    def grad_copy(sign, k, block):
+        out, inbox = (out_dn, in_dn) if sign else (out_up, in_up)
+        send, recv = (d_send, d_recv) if sign else (u_send, u_recv)
+        return remote(out.at[k], inbox.at[block], send.at[k], recv.at[k], owner(k, sign))
+
+    def to_relay(sign):
+        out, send = (out_dn, d_send) if sign else (out_up, u_send)
+        to = lax.rem(z + (4 if sign else 12), LANGS)
+        return remote(out.at[0], relay.at[sign], send.at[0], r_recv.at[sign], to)
+
+    def from_relay(sign):
+        inbox, recv = (in_dn, d_recv) if sign else (in_up, u_recv)
+        source, to = lax.rem(z + (12 if sign else 4), LANGS), lax.rem(z + (4 if sign else 12), LANGS)
+        return remote(relay.at[sign], inbox.at[source], r_send.at[sign], recv.at[0], to)
+
+    out_dn[0] = down(0)
+    to_relay(1).start()
+
+    @pl.loop(1, EARLY)
     def _(k):
         out_dn[k] = down(k)
-        grad_copy(out_dn, in_dn, k, z, d_send, d_recv).start()
+        grad_copy(1, k, z).start()
 
     for roles in ARRIVALS:
         rest.step(roles)
@@ -349,7 +363,7 @@
     @pl.loop(EARLY, LANGS - 1)
     def _(k):
         out_dn[k] = down(k)
-        grad_copy(out_dn, in_dn, k, z, d_send, d_recv).start()
+        grad_copy(1, k, z).start()
 
     in_dn[z] = down(LANGS - 1)
 
@@ -368,24 +382,37 @@
             preferred_element_type=jnp.float32,
         ).astype(jnp.bfloat16)
 
-    @pl.loop(0, LANGS - 1)
+    to_relay(1).wait_recv()
+    from_relay(1).start()
+    out_up[0] = up(owner(0, 0))
+    to_relay(0).start()
+
+    @pl.loop(1, 7)
     def _(k):
-        out_up[k] = up(owner(k))
-        grad_copy(out_up, in_up, k, z, u_send, u_recv).start()
+        out_up[k] = up(owner(k, 0))
+        grad_copy(0, k, z).start()
 
     in_up[z] = up(z)
+    to_relay(0).wait_recv()
+    from_relay(0).start()
+
+    @pl.loop(7, LANGS - 1)
+    def _(k):
+        out_up[k] = up(owner(k, 0))
+        grad_copy(0, k, z).start()
 
     for copy in tokens.started + first.started + rest.started:
         copy.wait_send()
 
     pairs[...] = jnp.zeros_like(pairs)
-
-    for inbox, out, send, recv in ((in_dn, out_dn, d_send, d_recv), (in_up, out_up, u_send, u_recv)):
+    targets_t = tgt[...].T
+    accept_t = acc[...].T
+
+    for sign, inbox in ((1, in_dn), (0, in_up)):
 
         @pl.loop(0, LANGS - 1)
         def _(k):
-            source = lax.rem(z + LANGS - distance_of(k), LANGS)
-            grad_copy(out, inbox, k, source, send, recv).wait_recv()
+            grad_copy(sign, k, lax.rem(z + LANGS - distance_of(k, sign), LANGS)).wait_recv()
 
         @pl.loop(0, 2)
         def _(g):
@@ -417,8 +444,8 @@
     sends += exchange(st3, "lang", LANGS, z, s3_send, s3_recv)
     gram = jnp.sum(st3[...], axis=0)[:, :LANGS]
 
-    weights, new_targets = vaccinate(gram, tgt[...], acc[...])
-    nt_out[...] = new_targets
+    weights, cos_pairs = vaccinate(gram, targets_t, accept_t)
+    nt_out[...] = (1.0 - ema_rate) * tgt[...] + ema_rate * cos_pairs
     wv[...] = jnp.broadcast_to(weights, (LANGS, DS))
 
     for inbox, half in ((in_up, 0), (in_dn, 1)):
@@ -441,14 +468,17 @@
 
     @pl.loop(0, LANGS - 1)
     def _(k):
-        grad_copy(out_dn, in_dn, k, z, d_send, d_recv).wait_send()
-        grad_copy(out_up, in_up, k, z, u_send, u_recv).wait_send()
+        grad_copy(1, k, z).wait_send()
+        grad_copy(0, k, z).wait_send()
+
+    from_relay(0).wait_send()
+    from_relay(1).wait_send()
 
 
 def on_device(tokens, cotangent, lengths, up_weight, down_weight, targets, accept):
     bf16, f32 = jnp.bfloat16, jnp.float32
     dma = pltpu.SemaphoreType.DMA
-    any_space = pl.BlockSpec(memory_space=pl.ANY)
+    hbm = pl.BlockSpec(memory_space=pl.ANY)
     vmem = pl.BlockSpec(memory_space=pltpu.VMEM)
     return pl.pallas_call(
         kernel,
@@ -457,7 +487,7 @@
             jax.ShapeDtypeStruct((HID, DS), f32),
             jax.ShapeDtypeStruct((LANGS, LANGS), f32),
         ),
-        in_specs=[any_space] * 7,
+        in_specs=[hbm] * 7,
         out_specs=(vmem, vmem, vmem),
         scratch_shapes=[
             pltpu.VMEM((2, 4, 4, ROWS, D), bf16),
@@ -476,6 +506,7 @@
             pltpu.VMEM((LANGS - 1, HID, DS), bf16),
             pltpu.VMEM((LANGS, HID, DS), bf16),
             pltpu.VMEM((LANGS, HID, DS), bf16),
+            pltpu.VMEM((2, HID, DS), bf16),
             pltpu.VMEM((256, 256), f32),
             pltpu.VMEM((NF, LANGS, 128), f32),
             pltpu.VMEM((NY, LANGS, 128), f32),
@@ -487,6 +518,7 @@
             dma((20,)), dma((32,)), dma((4,)), dma((4,)),
             dma((20,)), dma((32,)), dma((4,)), dma((4,)),
             dma((LANGS - 1,)), dma((LANGS - 1,)), dma((LANGS - 1,)), dma((LANGS - 1,)),
+            dma((2,)), dma((2,)),
             dma((NF,)), dma((NF,)), dma((NY,)), dma((NY,)), dma((LANGS,)), dma((LANGS,)),
         ],
         compiler_params=pltpu.CompilerParams(

time: 167 us -> 164 us (0.982)
  Pallas kernels: 162 us -> 159 us
    pallas_call x1, Pallas kernels: 162 us -> 159 us  [on_device(): pl.pallas_call(kernel, out_shape=(jax.ShapeDtypeStruct((DS, HID), f32), j...]
where the time goes in v3:
time: 164 us; the launch traced here: 163 us
  Pallas kernels  159 us (97%)
  local copies, waits for them, and re-layouts  2.9 us (2%)
    pallas_call x1, Pallas kernels, on_device(): pl.pallas_call(kernel, out_shape=(jax.ShapeDtypeStruct((DS, HID), f32), j...  159 us

profile of v3, /device:TPU:1, one launch (start us, length us, event | category | flops | bytes accessed | tf_op | source)
XLA Modules:
  0.0 162.6 jit_solution(4462838447353101068)
XLA Ops:
  0.6 159.1 %vaccine_step.1 = (f32[128,256]{1,0:T(8,128)}, f32[256,128]{1,0:T(8,128)}, f32[16,16]{1,0:T(8,128)}) custom-call(bf16[1,48,2048]{2,1,0:T(8,128)(2,1)} %tok_ref.1, bf16[1,48,2048]{2,1,0:T(8,128)(2,1)} %cot_ref.1, s32[1,12]{1,0:T(1,128)} %len_hbm.1, bf16[2048,256]{1,0:T(8,128)(2,1)} %wup_hbm.1, bf16[256,2048]{1,0:T(8,128)(2,1)} %wdn_hbm.1, f32[16,16]{1,0:T(8,128)} %tgt_hbm.1, ...), custom_call_target="tpu_custom_call" | custom-call | flops 6442450944 | bytes 4194304 | tf_op jit(solution)/shard_map/vaccine_step/pallas_call | solution.py:483
  159.7 0.0 copy-start
  159.7 1.6 copy.13
  161.3 0.0 copy-done
  161.3 0.0 copy-start.1
  161.3 0.7 copy.14
  162.0 0.0 copy-done.1
  162.0 0.6 copy.15
Async XLA Ops:
  159.7 1.6 copy-start
  161.3 0.7 copy-start.1

commit v4 on v3

--- a/solution.py
+++ b/solution.py
@@ -198,15 +198,15 @@
 
 
 def kernel(
-    tok_ref, cot_ref, len_hbm, wup_hbm, wdn_hbm, tgt_hbm, acc_hbm,
-    up_out, dn_out, nt_out,
-    x_buf, c_buf, wup, wdn, wdn_t, tgt, acc, lens, v_buf, hp, h_t, p_t,
-    out_dn, out_up, in_dn, in_up, relay, pairs, st1, st2, st3, wv, comb,
+    tok_ref, cot_ref, len_hbm, wup_hbm, wdn_hbm,
+    up_out, dn_out, gram_out,
+    x_buf, c_buf, wup, wdn, wdn_t, lens, v_buf, hp, h_t, p_t,
+    out_dn, out_up, in_dn, in_up, relay, pairs,
     local_sem, cols_sem,
     t_send, t_recv, t_sib_send, t_sib_recv,
     e_send, e_recv, e_sib_send, e_sib_recv,
     l_send, l_recv, l_sib_send, l_sib_recv,
-    d_send, d_recv, u_send, u_recv, r_send, r_recv, s1_send, s1_recv, s2_send, s2_recv, s3_send, s3_recv,
+    d_send, d_recv, u_send, u_recv, r_send, r_recv,
 ):
     z, y, f = lax.axis_index("lang"), lax.axis_index("dp"), lax.axis_index("fsdp")
     x, core = f // 2, lax.rem(f, 2)
@@ -236,9 +236,7 @@
         pltpu.make_async_copy(tok, x_buf.at[0, 0, 0], local_sem.at[0]),
         pltpu.make_async_copy(wdn_hbm, wdn, local_sem.at[1]),
         pltpu.make_async_copy(wup_hbm, wup, local_sem.at[2]),
-        pltpu.make_async_copy(tgt_hbm, tgt, local_sem.at[3]),
-        pltpu.make_async_copy(acc_hbm, acc, local_sem.at[4]),
-        pltpu.make_async_copy(len_hbm, lens, local_sem.at[5]),
+        pltpu.make_async_copy(len_hbm, lens, local_sem.at[3]),
     ]
     for copy in cot_copies + local:
         copy.start()
@@ -262,8 +260,11 @@
     for copy in local:
         copy.wait()
 
-    for k in range(LANGS):
-        wdn_t[pl.ds(k * DS, DS), :] = wdn[:, columns(owner(k, 1))].T
+    wdn_t[pl.ds((LANGS - 1) * DS, DS), :] = wdn[:, columns(z)].T
+
+    @pl.loop(0, LANGS - 1)
+    def _(k):
+        wdn_t[pl.ds(pl.multiple_of(k * DS, DS), DS), :] = wdn[:, columns(owner(k, 1))].T
 
     def activate(which, second):
         base = (which * 4 + second) * 192
@@ -367,13 +368,15 @@
 
     in_dn[z] = down(LANGS - 1)
 
-    for group in range(8):
+    @pl.loop(0, 4)
+    def _(pair):
+        which, second = pair // 2, 2 * lax.rem(pair, 2)
         hg = jnp.dot(
-            c_buf[group // 4, group % 4].reshape(192, D), wdn_t[...], preferred_element_type=jnp.float32
-        )
-        rows = pl.ds(group * 192, 192)
-        hp[rows, :] = (hg * v_buf[rows, :]).astype(jnp.bfloat16)
-    turn(p_t, 0, 12)
+            c_buf[which, pl.ds(second, 2)].reshape(384, D), wdn_t[...], preferred_element_type=jnp.float32
+        )
+        rows = pl.ds(pl.multiple_of(pair * 384, 128), 384)
+        p = (hg * v_buf[rows, :]).astype(jnp.bfloat16)
+        p_t[:, rows] = p.T
 
     def up(block):
         return jnp.dot(
@@ -405,14 +408,18 @@
         copy.wait_send()
 
     pairs[...] = jnp.zeros_like(pairs)
-    targets_t = tgt[...].T
-    accept_t = acc[...].T
+    keep = [
+        pltpu.make_async_copy(in_dn, dn_out, local_sem.at[4]),
+        pltpu.make_async_copy(in_up, up_out, local_sem.at[5]),
+    ]
 
     for sign, inbox in ((1, in_dn), (0, in_up)):
 
         @pl.loop(0, LANGS - 1)
         def _(k):
             grad_copy(sign, k, lax.rem(z + LANGS - distance_of(k, sign), LANGS)).wait_recv()
+
+        keep[1 - sign].start()
 
         @pl.loop(0, 2)
         def _(g):
@@ -434,23 +441,53 @@
     li = lax.broadcasted_iota(jnp.int32, (256, 128), 0) // 16
     lj = lax.broadcasted_iota(jnp.int32, (256, 128), 1)
     select = (li == lj).astype(jnp.float32)
-    st1[f] = jnp.dot(
+    gram_out[...] = jnp.dot(
         by_row, select, precision=lax.Precision.HIGHEST, preferred_element_type=jnp.float32
     )
+    for copy in keep:
+        copy.wait()
+
+    @pl.loop(0, LANGS - 1)
+    def _(k):
+        grad_copy(1, k, z).wait_send()
+        grad_copy(0, k, z).wait_send()
+
+    from_relay(0).wait_send()
+    from_relay(1).wait_send()
+
+
+def project(
+    part_ref, tgt, acc, weights_out, nt_out, st1, st2, st3,
+    s1_send, s1_recv, s2_send, s2_recv, s3_send, s3_recv,
+):
+    z, y, f = lax.axis_index("lang"), lax.axis_index("dp"), lax.axis_index("fsdp")
+    barrier = pltpu.get_barrier_semaphore()
+    for axis, count, me in (("fsdp", NF, f), ("dp", NY, y), ("lang", LANGS, z)):
+        for r in range(1, count):
+            pl.semaphore_signal(
+                barrier, inc=1, device_id={axis: lax.rem(me + r, count)}, device_id_type=MESH
+            )
+    targets_t = tgt[...].T
+    accept_t = acc[...].T
+    st1[f] = part_ref[...]
+    pl.semaphore_wait(barrier, (NF - 1) + (NY - 1) + (LANGS - 1))
     sends = exchange(st1, "fsdp", NF, f, s1_send, s1_recv)
     st2[y] = jnp.sum(st1[...], axis=0)
     sends += exchange(st2, "dp", NY, y, s2_send, s2_recv)
     st3[z] = jnp.sum(st2[...], axis=0)
     sends += exchange(st3, "lang", LANGS, z, s3_send, s3_recv)
     gram = jnp.sum(st3[...], axis=0)[:, :LANGS]
-
     weights, cos_pairs = vaccinate(gram, targets_t, accept_t)
     nt_out[...] = (1.0 - ema_rate) * tgt[...] + ema_rate * cos_pairs
-    wv[...] = jnp.broadcast_to(weights, (LANGS, DS))
-
-    for inbox, half in ((in_up, 0), (in_dn, 1)):
-
-        @pl.loop(0, 4)
+    weights_out[...] = jnp.broadcast_to(weights, (LANGS, DS))
+    for copy in sends:
+        copy.wait_send()
+
+
+def combine(up_ref, dn_ref, wv, up_out, dn_out, comb):
+    for inbox, half in ((up_ref, 0), (dn_ref, 1)):
+
+        @pl.loop(0, 2)
         def _(r):
             rows = pl.ds(pl.multiple_of(r * 64, 64), 64)
             total = jnp.zeros((64, DS), jnp.float32)
@@ -463,40 +500,27 @@
 
     up_out[...] = comb[...].T
 
-    for copy in sends:
-        copy.wait_send()
-
-    @pl.loop(0, LANGS - 1)
-    def _(k):
-        grad_copy(1, k, z).wait_send()
-        grad_copy(0, k, z).wait_send()
-
-    from_relay(0).wait_send()
-    from_relay(1).wait_send()
-
 
 def on_device(tokens, cotangent, lengths, up_weight, down_weight, targets, accept):
     bf16, f32 = jnp.bfloat16, jnp.float32
     dma = pltpu.SemaphoreType.DMA
     hbm = pl.BlockSpec(memory_space=pl.ANY)
     vmem = pl.BlockSpec(memory_space=pltpu.VMEM)
-    return pl.pallas_call(
+    up_parts, dn_parts, part = pl.pallas_call(
         kernel,
         out_shape=(
-            jax.ShapeDtypeStruct((DS, HID), f32),
-            jax.ShapeDtypeStruct((HID, DS), f32),
-            jax.ShapeDtypeStruct((LANGS, LANGS), f32),
+            jax.ShapeDtypeStruct((LANGS, HID, DS), bf16),
+            jax.ShapeDtypeStruct((LANGS, HID, DS), bf16),
+            jax.ShapeDtypeStruct((LANGS, 128), f32),
         ),
-        in_specs=[hbm] * 7,
-        out_specs=(vmem, vmem, vmem),
+        in_specs=[hbm] * 5,
+        out_specs=(hbm, hbm, vmem),
         scratch_shapes=[
             pltpu.VMEM((2, 4, 4, ROWS, D), bf16),
             pltpu.VMEM((2, 4, 4, ROWS, D), bf16),
             pltpu.VMEM((D, HID), bf16),
             pltpu.VMEM((HID, D), bf16),
             pltpu.VMEM((D, HID), bf16),
-            pltpu.VMEM((LANGS, LANGS), f32),
-            pltpu.VMEM((LANGS, LANGS), jnp.int32),
             pltpu.SMEM((1, 12), jnp.int32),
             pltpu.VMEM((LTOK, HID), f32),
             pltpu.VMEM((LTOK, HID), bf16),
@@ -508,18 +532,12 @@
             pltpu.VMEM((LANGS, HID, DS), bf16),
             pltpu.VMEM((2, HID, DS), bf16),
             pltpu.VMEM((256, 256), f32),
-            pltpu.VMEM((NF, LANGS, 128), f32),
-            pltpu.VMEM((NY, LANGS, 128), f32),
-            pltpu.VMEM((LANGS, LANGS, 128), f32),
-            pltpu.VMEM((LANGS, DS), f32),
-            pltpu.VMEM((HID, DS), f32),
             dma((6,)), dma((LANGS,)),
             dma((20,)), dma((32,)), dma((4,)), dma((4,)),
             dma((20,)), dma((32,)), dma((4,)), dma((4,)),
             dma((20,)), dma((32,)), dma((4,)), dma((4,)),
             dma((LANGS - 1,)), dma((LANGS - 1,)), dma((LANGS - 1,)), dma((LANGS - 1,)),
             dma((2,)), dma((2,)),
-            dma((NF,)), dma((NF,)), dma((NY,)), dma((NY,)), dma((LANGS,)), dma((LANGS,)),
         ],
         compiler_params=pltpu.CompilerParams(
             collective_id=0, has_side_effects=True, vmem_limit_bytes=60 * 1024 * 1024
@@ -527,8 +545,40 @@
         cost_estimate=pl.CostEstimate(
             flops=4 * 2 * LTOK * D * HID, bytes_accessed=4 * 1024 * 1024, transcendentals=LTOK * HID
         ),
-        name="vaccine_step",
-    )(tokens, cotangent, lengths, up_weight, down_weight, targets, accept)
+        name="grads",
+    )(tokens, cotangent, lengths, up_weight, down_weight)
+    weights, new_targets = pl.pallas_call(
+        project,
+        out_shape=(jax.ShapeDtypeStruct((LANGS, DS), f32), jax.ShapeDtypeStruct((LANGS, LANGS), f32)),
+        in_specs=[vmem] * 3,
+        out_specs=(vmem, vmem),
+        scratch_shapes=[
+            pltpu.VMEM((NF, LANGS, 128), f32),
+            pltpu.VMEM((NY, LANGS, 128), f32),
+            pltpu.VMEM((LANGS, LANGS, 128), f32),
+            dma((NF,)), dma((NF,)), dma((NY,)), dma((NY,)), dma((LANGS,)), dma((LANGS,)),
+        ],
+        compiler_params=pltpu.CompilerParams(collective_id=1, has_side_effects=True),
+        name="project",
+    )(part, targets, accept)
+    up_update, down_update = pl.pallas_call(
+        combine,
+        out_shape=(jax.ShapeDtypeStruct((DS, HID), f32), jax.ShapeDtypeStruct((HID, DS), f32)),
+        grid=(2,),
+        in_specs=[
+            pl.BlockSpec((LANGS, 128, DS), lambda i: (0, i, 0)),
+            pl.BlockSpec((LANGS, 128, DS), lambda i: (0, i, 0)),
+            pl.BlockSpec((LANGS, DS), lambda i: (0, 0)),
+        ],
+        out_specs=(
+            pl.BlockSpec((DS, 128), lambda i: (0, i)),
+            pl.BlockSpec((128, DS), lambda i: (i, 0)),
+        ),
+        scratch_shapes=[pltpu.VMEM((128, DS), f32)],
+        compiler_params=pltpu.CompilerParams(vmem_limit_bytes=60 * 1024 * 1024),
+        name="combine",
+    )(up_parts, dn_parts, weights)
+    return up_update, down_update, new_targets
 
 
 def solution(mesh):

time: 164 us -> 171 us (1.043)
  Pallas kernels: 159 us -> 168 us
  local copies, waits for them, and re-layouts: 2.9 us -> 0.6 us
    pallas_call x1 -> x3, Pallas kernels: 159 us -> 168 us  [the longest x1 143 us: on_device(): pl.pallas_call(kernel, out_shape=(jax.ShapeDtypeStruct((LANGS, HID, DS),...]
    unnamed x7 -> x3, local copies, waits for them, and re-layouts: 2.9 us -> 0.6 us
where the time goes in v4:
time: 171 us; the launch traced here: 169 us
  Pallas kernels  168 us (98%)
    pallas_call x1, Pallas kernels, on_device(): pl.pallas_call(kernel, out_shape=(jax.ShapeDtypeStruct((LANGS, HID, DS),...  143 us
    pallas_call x1, Pallas kernels, on_device(): pl.pallas_call(project, out_shape=(jax.ShapeDtypeStruct((LANGS, DS), f32)...  21.9 us

profile of v4, /device:TPU:1, one launch (start us, length us, event | category | flops | bytes accessed | tf_op | source)
XLA Modules:
  0.0 169.2 jit_solution(7978731107709129137)
XLA Ops:
  0.6 143.5 %grads.1 = (bf16[16,256,128]{2,1,0:T(8,128)(2,1)}, bf16[16,256,128]{2,1,0:T(8,128)(2,1)}, f32[16,128]{1,0:T(8,128)}) custom-call(bf16[1,48,2048]{2,1,0:T(8,128)(2,1)} %tok_ref.1, bf16[1,48,2048]{2,1,0:T(8,128)(2,1)} %cot_ref.1, s32[1,12]{1,0:T(1,128)} %len_hbm.1, bf16[2048,256]{1,0:T(8,128)(2,1)} %wup_hbm.1, bf16[256,2048]{1,0:T(8,128)(2,1)} %wdn_hbm.1), custom_call_target="tpu_custom_call" | custom-call | flops 6442450944 | bytes 4194304 | tf_op jit(solution)/shard_map/grads/pallas_call | solution.py:509
  144.1 21.9 %project.1 = (f32[16,128]{1,0:T(8,128)}, f32[16,16]{1,0:T(8,128)}) custom-call(f32[16,128]{1,0:T(8,128)} %get-tuple-element.12.part_ref, f32[16,16]{1,0:T(8,128)} %tgt.1, s32[16,16]{1,0:T(8,128)} %acc.1), custom_call_target="tpu_custom_call" | custom-call | tf_op jit(solution)/shard_map/project/pallas_call | solution.py:550
  166.1 0.0 copy-start
  166.1 2.5 %combine.1 = (f32[128,256]{1,0:T(8,128)}, f32[256,128]{1,0:T(8,128)}) custom-call(bf16[16,256,128]{2,1,0:T(8,128)(2,1)} %get-tuple-element.10.up_ref, bf16[16,256,128]{2,1,0:T(8,128)(2,1)} %get-tuple-element.11.dn_ref, f32[16,128]{1,0:T(8,128)} %get-tuple-element.13.wv), custom_call_target="tpu_custom_call" | custom-call | tf_op jit(solution)/shard_map/combine/pallas_call | solution.py:564
  168.6 0.0 copy-done
  168.6 0.6 copy.11
Async XLA Ops:
  166.1 2.6 %copy-start = (f32[16,16]{1,0:T(8,128)S(1)}, f32[16,16]{1,0:T(8,128)}, u32[]{:S(2)}) copy-start(f32[16,16]{1,0:T(8,128)} %get-tuple-element.22) | copy-start | bytes 3076

commit v5 on v2

--- a/solution.py
+++ b/solution.py
@@ -44,12 +44,6 @@
                     "fsdp": lax.rem(x + dx, 4) * 2 + core,
                 }
         self.sibling = {"fsdp": x * 2 + (1 - core)}
-
-    def first_token(self, which, second, first):
-        core = self.core if which == 0 else 1 - self.core
-        dx = jnp.where(core == 0, OFFSETS[first], OFFSETS[second])
-        dy = OFFSETS[first] + OFFSETS[second] - dx
-        return (lax.rem(self.y + dy, 4) * NF + lax.rem(self.x + dx, 4) * 2 + core) * ROWS
 
 
 class Gather:
@@ -133,9 +127,9 @@
             self.to_sibling(roles[0])
 
 
-def distance_of(k):
-    m = 8 - (k + 1) // 2
-    return jnp.where(lax.rem(k, 2) == 1, m, LANGS - m)
+def distance_of(k, sign):
+    m = 4 - (k + 1) // 2
+    return jnp.where(lax.rem(k + sign, 2) == 1, LANGS - m, m)
 
 
 def exchange(buf, axis, count, me, send, recv):
@@ -164,48 +158,47 @@
     return copies
 
 
-def vaccinate(gram, targets, accept):
+def vaccinate(gram, targets_t, accept_t):
     rows = lax.broadcasted_iota(jnp.int32, (LANGS, LANGS), 0)
     cols = lax.broadcasted_iota(jnp.int32, (LANGS, LANGS), 1)
     identity = (rows == cols).astype(jnp.float32)
-    allowed = accept.astype(jnp.float32) * (1.0 - identity)
+    roots = jnp.sqrt(1.0 - targets_t * targets_t)
     diag_col = jnp.sum(gram * identity, axis=1, keepdims=True)
     diag_row = jnp.sum(gram * identity, axis=0, keepdims=True)
     cos_pairs = gram / jnp.sqrt(diag_col * diag_row)
-    roots = jnp.sqrt(1.0 - targets * targets)
+    inverse = 1.0 / jnp.sqrt(diag_col)
+    scale = inverse / roots
+    allowed = accept_t.astype(jnp.float32) * (1.0 - identity)
     coeffs, product = identity, gram
     for j in range(LANGS):
-        inner = product[:, j : j + 1]
-        norm_sq = jnp.sum(product * coeffs, axis=1, keepdims=True)
-        own = gram[j : j + 1, j : j + 1]
-        cosine = inner / jnp.sqrt(norm_sq * own)
-        root = roots[:, j : j + 1]
+        norm_sq = jnp.sum(product * coeffs, axis=0, keepdims=True)
+        over_norm = lax.rsqrt(norm_sq)
+        cosine = product[j : j + 1, :] * inverse[j : j + 1, :] * over_norm
         sine = jnp.sqrt(jnp.maximum(1.0 - cosine * cosine, 0.0))
         step = (
-            jnp.sqrt(norm_sq) * (targets[:, j : j + 1] * sine - cosine * root) / (jnp.sqrt(own) * root)
-        )
-        step = jnp.where(allowed[:, j : j + 1] > 0.5, step, 0.0)
-        coeffs = coeffs + step * identity[j : j + 1, :]
-        product = product + step * gram[j : j + 1, :]
-    weights_row = jnp.sum(coeffs, axis=0, keepdims=True)
-    weights_col = jnp.sum(identity * weights_row, axis=1, keepdims=True)
-    quad = jnp.sum(weights_col * gram * weights_row, axis=(0, 1), keepdims=True)
+            (norm_sq * over_norm)
+            * (targets_t[j : j + 1, :] * sine - cosine * roots[j : j + 1, :])
+            * scale[j : j + 1, :]
+        )
+        step = jnp.where(allowed[j : j + 1, :] > 0.5, step, 0.0)
+        coeffs = jnp.where(rows == j, coeffs + step, coeffs)
+        product = product + gram[:, j : j + 1] * step
+    weights = jnp.sum(coeffs, axis=1, keepdims=True)
+    along = jnp.sum(product, axis=1, keepdims=True)
+    quad = jnp.sum(weights * along, axis=0, keepdims=True)
     mean_square = jnp.maximum(quad, 0.0) / (2.0 * D * FF)
     factor = jnp.minimum(1.0, clip_level / jnp.sqrt(mean_square + 1e-06))
-    new_targets = (1.0 - ema_rate) * targets + ema_rate * cos_pairs
-    return weights_col * factor, new_targets
+    return weights * factor, cos_pairs
 
 
 def kernel(
     tok_ref, cot_ref, len_hbm, wup_hbm, wdn_hbm, tgt_hbm, acc_hbm,
     up_out, dn_out, nt_out,
-    x_buf, c_buf, wup, wdn, wdn_t, tgt, acc, lens, v_buf, hp, h_t, p_t,
-    out_dn, out_up, in_dn, in_up, pairs, st1, st2, st3, wv, comb,
-    local_sem, cols_sem,
-    t_send, t_recv, t_sib_send, t_sib_recv,
-    e_send, e_recv, e_sib_send, e_sib_recv,
-    l_send, l_recv, l_sib_send, l_sib_recv,
-    d_send, d_recv, u_send, u_recv, s1_send, s1_recv, s2_send, s2_recv, s3_send, s3_recv,
+    x_buf, c_buf, x_two, c_two, wup, wdn, wdn_t, tgt, acc, lens, v_buf, hp, h_t, p_t,
+    out_dn, out_up, in_dn, in_up, relay, pairs, st1, st2, st3, wv, comb,
+    local_sem, cols_sem, sems,
+    d_send, d_recv, u_send, u_recv, i_send, i_recv, r_send, r_recv,
+    s1_send, s1_recv, s2_send, s2_recv, s3_send, s3_recv,
 ):
     z, y, f = lax.axis_index("lang"), lax.axis_index("dp"), lax.axis_index("fsdp")
     x, core = f // 2, lax.rem(f, 2)
@@ -217,175 +210,278 @@
                 barrier, inc=1, device_id={axis: lax.rem(me + r, count)}, device_id_type=MESH
             )
 
-    def owner(k):
-        return lax.rem(z + (distance_of(k) if not isinstance(k, int) or k < 15 else 0), LANGS)
+    def owner(k, sign):
+        return lax.rem(z + distance_of(k, sign), LANGS)
 
     def columns(block):
         return pl.ds(pl.multiple_of(block * DS, DS), DS)
+
+    def source_columns(k):
+        return columns(owner(k, 1) if k < 8 else lax.rem(owner(k - 8, 1) + 8, LANGS))
 
     plane = Plane(x, y, core)
     tok, cot = tok_ref.at[0], cot_ref.at[0]
     cot_copies = [
         pltpu.make_async_copy(
-            cot.at[:, columns(owner(k))], c_buf.at[0, 0, 0, :, pl.ds(k * DS, DS)], cols_sem.at[k]
+            cot.at[:, source_columns(k)], c_buf.at[0, 0, 0, :, pl.ds(k * DS, DS)], cols_sem.at[k]
         )
         for k in range(LANGS)
     ]
+    lens_copy = pltpu.make_async_copy(len_hbm, lens, local_sem.at[5])
     local = [
         pltpu.make_async_copy(tok, x_buf.at[0, 0, 0], local_sem.at[0]),
         pltpu.make_async_copy(wdn_hbm, wdn, local_sem.at[1]),
         pltpu.make_async_copy(wup_hbm, wup, local_sem.at[2]),
         pltpu.make_async_copy(tgt_hbm, tgt, local_sem.at[3]),
         pltpu.make_async_copy(acc_hbm, acc, local_sem.at[4]),
-        pltpu.make_async_copy(len_hbm, lens, local_sem.at[5]),
     ]
+    lens_copy.start()
     for copy in cot_copies + local:
         copy.start()
 
     early = EARLY * DS
-    tokens = Gather(plane, tok, x_buf, 0, D, t_send, t_recv, t_sib_send, t_sib_recv)
-    first = Gather(
-        plane, c_buf.at[0, 0, 0, :, pl.ds(0, early)], c_buf, 0, early,
-        e_send, e_recv, e_sib_send, e_sib_recv,
-    )
-    rest = Gather(
-        plane, c_buf.at[0, 0, 0, :, pl.ds(early, D - early)], c_buf, early, D - early,
-        l_send, l_recv, l_sib_send, l_sib_recv,
-    )
+
+    def gathers(number, own, x_ref, c_ref):
+        made = []
+        for n, (src, buf, start, width) in enumerate(
+            (
+                (own, x_ref, 0, D),
+                (c_ref.at[0, 0, 0, :, pl.ds(0, early)], c_ref, 0, early),
+                (c_ref.at[0, 0, 0, :, pl.ds(early, D - early)], c_ref, early, D - early),
+            )
+        ):
+            base = (3 * number + n) * 60
+            parts = [sems.at[pl.ds(base + a, b)] for a, b in ((0, 20), (20, 32), (52, 4), (56, 4))]
+            made.append(Gather(plane, src, buf, start, width, *parts))
+        return made
+
+    tokens, first, rest = gathers(0, tok, x_buf, c_buf)
+    tokens2, first2, rest2 = gathers(1, x_two.at[0, 0, 0], x_two, c_two)
+
+    def remote(src, dst, send, recv, to):
+        return pltpu.make_async_remote_copy(
+            src_ref=src, dst_ref=dst, send_sem=send, recv_sem=recv, device_id={"lang": to}, device_id_type=MESH
+        )
+
+    def columns_half(ref, n):
+        return ref.at[:, pl.ds(n * HALF, HALF)]
+
+    def leg_to(n):
+        return lax.rem(z + (4 if n % 2 == 0 else 12), LANGS)
+
+    def first_leg(n):
+        src = columns_half(tok if n < 2 else c_buf.at[0, 0, 0], n % 2)
+        return remote(src, relay.at[n], i_send.at[n], i_recv.at[n], leg_to(n))
+
+    def second_leg(n):
+        dst = columns_half(x_two.at[0, 0, 0], n) if n < 2 else columns_half(c_two.at[0, 0, 0], 3 - n)
+        return remote(relay.at[n], dst, r_send.at[n], r_recv.at[n], leg_to(n))
+
+    def forward(n):
+        first_leg(n).wait_recv()
+        second_leg(n).start()
 
     pl.semaphore_wait(barrier, (NF - 1) + (NY - 1) + (LANGS - 1))
     tokens.ready((0, 0))
+    first_leg(0).start()
+    first_leg(1).start()
+
+    lens_copy.wait()
     for copy in cot_copies:
         copy.wait()
+    token = (y * NF + x * 2 + core) * ROWS
+    slot = token // SEQ
+    here, after = lens[0, slot], lens[0, jnp.minimum(slot + 1, 11)]
+    place = lax.broadcasted_iota(jnp.int32, (ROWS, D), 0) + (token - slot * SEQ)
+    kept = place < jnp.where(place < SEQ, here, after + SEQ)
+    mine = c_buf[0, 0, 0].astype(jnp.float32)
+    c_buf[0, 0, 0] = jnp.where(kept, mine, 0.0).astype(jnp.bfloat16)
     first.ready((0, 0))
+    first_leg(2).start()
+    first_leg(3).start()
+
     for copy in local:
         copy.wait()
 
-    for k in range(LANGS):
-        wdn_t[pl.ds(k * DS, DS), :] = wdn[:, columns(owner(k))].T
-
-    def activate(which, second):
+    @pl.loop(0, 8)
+    def _(k):
+        low = owner(k, 1)
+        wdn_t[pl.ds(pl.multiple_of(k * DS, DS), DS), :] = wdn[:, columns(low)].T
+        high = lax.rem(low + 8, LANGS)
+        wdn_t[pl.ds(pl.multiple_of(HALF + k * DS, DS), DS), :] = wdn[:, columns(high)].T
+
+    def activate(x_ref, which, second):
         base = (which * 4 + second) * 192
         v_buf[pl.ds(base, 192), :] = jnp.dot(
-            x_buf[which, second].reshape(192, D), wup[...], preferred_element_type=jnp.float32
-        )
-        for i in range(4):
-            token = plane.first_token(which, second, i)
-            slot = token // SEQ
-            offset = token - slot * SEQ
-            here, after = lens[0, slot], lens[0, jnp.minimum(slot + 1, 11)]
-            place = lax.broadcasted_iota(jnp.int32, (ROWS, HID), 0) + offset
-            keep = place < jnp.where(place < SEQ, here, after + SEQ)
-            rows = pl.ds(base + i * ROWS, ROWS)
+            x_ref[which, second].reshape(192, D), wup[...], preferred_element_type=jnp.float32
+        )
+
+        @pl.loop(0, 4)
+        def _(i):
+            rows = pl.ds(pl.multiple_of(base + i * ROWS, 16), ROWS)
             v = v_buf[rows, :]
             k = 0.7978845608028654
             sq = v * v
             t = jnp.tanh(k * (v + 0.044715 * (sq * v)))
             cdf = 0.5 * (1.0 + t)
-            slope = cdf + 0.5 * v * (1.0 - t * t) * (k * (1.0 + 3.0 * 0.044715 * sq))
-            hp[rows, :] = jnp.where(keep, v * cdf, 0.0).astype(jnp.bfloat16)
-            v_buf[rows, :] = jnp.where(keep, slope, 0.0)
+            v_buf[rows, :] = cdf + 0.5 * v * (1.0 - t * t) * (k * (1.0 + 3.0 * 0.044715 * sq))
+            hp[rows, :] = (v * cdf).astype(jnp.bfloat16)
 
     def turn(dst, start, count):
-        for i in range(start, start + count):
-            dst[:, pl.ds(i * 128, 128)] = hp[pl.ds(i * 128, 128), :].T
-
-    for n, roles in enumerate(ARRIVALS):
-        tokens.step(roles)
-        first.step(roles)
-        if roles == (2, 1):
-            tokens.from_sibling(0)
-            activate(0, 0)
-            rest.ready((0, 0))
-        elif roles == (2, 2):
-            activate(1, 0)
-        elif roles == (2, 3):
-            activate(0, 1)
-        elif roles == (3, 0):
-            tokens.from_sibling(1)
-            activate(1, 1)
-        elif roles == (3, 1):
-            activate(0, 2)
-        elif roles == (3, 2):
-            tokens.from_sibling(2)
-            activate(1, 2)
-    turn(h_t, 0, 3)
-    turn(h_t, 6, 3)
-    activate(0, 3)
-    tokens.from_sibling(3)
-    activate(1, 3)
-    turn(h_t, 3, 3)
-    turn(h_t, 9, 3)
-    for second in range(4):
-        first.from_sibling(second)
-
-    def down(k):
+        @pl.loop(start, start + count)
+        def _(i):
+            part = pl.ds(pl.multiple_of(i * 128, 128), 128)
+            dst[:, part] = hp[part, :].T
+
+    def down(c_ref, k):
         return jnp.dot(
             h_t[...],
-            c_buf[:, :, :, :, columns(k)].reshape(LTOK, DS),
+            c_ref[:, :, :, :, columns(k)].reshape(LTOK, DS),
             preferred_element_type=jnp.float32,
         ).astype(jnp.bfloat16)
 
-    def grad_copy(out, inbox, k, block, send, recv):
-        return pltpu.make_async_remote_copy(
-            src_ref=out.at[k],
-            dst_ref=inbox.at[block],
-            send_sem=send.at[k],
-            recv_sem=recv.at[k],
-            device_id={"lang": owner(k)},
-            device_id_type=MESH,
-        )
-
-    @pl.loop(0, EARLY)
-    def _(k):
-        out_dn[k] = down(k)
-        grad_copy(out_dn, in_dn, k, z, d_send, d_recv).start()
-
-    for roles in ARRIVALS:
+    def up(x_ref, k):
+        return jnp.dot(
+            p_t[...],
+            x_ref[:, :, :, :, columns(owner(k, 0))].reshape(LTOK, DS),
+            preferred_element_type=jnp.float32,
+        ).astype(jnp.bfloat16)
+
+    def grad_copy(sign, number, k, source):
+        out, inbox = (out_dn, in_dn) if sign else (out_up, in_up)
+        send, recv = (d_send, d_recv) if sign else (u_send, u_recv)
+        index = number * 7 + k
+        return remote(
+            out.at[index],
+            inbox.at[lax.rem(source + 8 * number, LANGS)],
+            send.at[index],
+            recv.at[index],
+            owner(k, sign),
+        )
+
+    def send_down(number, c_ref, start, stop):
+        @pl.loop(start, stop)
+        def _(k):
+            out_dn[number * 7 + k] = down(c_ref, k)
+            grad_copy(1, number, k, z).start()
+
+    def send_up(number, x_ref, start, stop):
+        @pl.loop(start, stop)
+        def _(k):
+            out_up[number * 7 + k] = up(x_ref, k)
+            grad_copy(0, number, k, z).start()
+
+    def preact_grad(c_ref, pair):
+        which, second = pair // 2, 2 * (pair % 2)
+        hg = jnp.dot(
+            c_ref[which, second : second + 2].reshape(384, D), wdn_t[...], preferred_element_type=jnp.float32
+        )
+        rows = pl.ds(pair * 384, 384)
+        hp[rows, :] = (hg * v_buf[rows, :]).astype(jnp.bfloat16)
+        turn(p_t, pair * 3, 3)
+
+    def with_tokens(gather_x, gather_c, x_ref, extra):
+        for n, roles in enumerate(ARRIVALS):
+            gather_x.step(roles)
+            gather_c.step(roles)
+            for piece in extra.get(n, ()):
+                piece()
+            if n == 8:
+                gather_x.from_sibling(0)
+                activate(x_ref, 0, 0)
+            elif n == 9:
+                activate(x_ref, 1, 0)
+            elif n == 10:
+                activate(x_ref, 0, 1)
+            elif n == 11:
+                gather_x.from_sibling(1)
+                activate(x_ref, 1, 1)
+            elif n == 12:
+                activate(x_ref, 0, 2)
+            elif n == 13:
+                gather_x.from_sibling(2)
+                activate(x_ref, 1, 2)
+        turn(h_t, 0, 3)
+        turn(h_t, 6, 3)
+        activate(x_ref, 0, 3)
+        gather_x.from_sibling(3)
+        activate(x_ref, 1, 3)
+        turn(h_t, 3, 3)
+        turn(h_t, 9, 3)
+        for second in range(4):
+            gather_c.from_sibling(second)
+
+    def begin_two():
+        second_leg(0).wait_recv()
+        second_leg(1).wait_recv()
+        tokens2.ready((0, 0))
+
+    with_tokens(
+        tokens, first, x_buf,
+        {
+            4: [lambda: rest.ready((0, 0))],
+            5: [lambda: forward(0), lambda: forward(1)],
+            10: [lambda: forward(2), lambda: forward(3)],
+        },
+    )
+    send_down(0, c_buf, 0, EARLY)
+    for n, roles in enumerate(ARRIVALS):
         rest.step(roles)
+        if n == 8:
+            begin_two()
+    second_leg(2).wait_recv()
+    second_leg(3).wait_recv()
+    first2.ready((0, 0))
     for second in range(4):
         rest.from_sibling(second)
-
-    @pl.loop(EARLY, LANGS - 1)
-    def _(k):
-        out_dn[k] = down(k)
-        grad_copy(out_dn, in_dn, k, z, d_send, d_recv).start()
-
-    in_dn[z] = down(LANGS - 1)
-
-    for group in range(8):
-        hg = jnp.dot(
-            c_buf[group // 4, group % 4].reshape(192, D), wdn_t[...], preferred_element_type=jnp.float32
-        )
-        rows = pl.ds(group * 192, 192)
-        hp[rows, :] = (hg * v_buf[rows, :]).astype(jnp.bfloat16)
-    turn(p_t, 0, 12)
-
-    def up(block):
-        return jnp.dot(
-            p_t[...],
-            x_buf[:, :, :, :, columns(block)].reshape(LTOK, DS),
-            preferred_element_type=jnp.float32,
-        ).astype(jnp.bfloat16)
-
-    @pl.loop(0, LANGS - 1)
-    def _(k):
-        out_up[k] = up(owner(k))
-        grad_copy(out_up, in_up, k, z, u_send, u_recv).start()
-
-    in_up[z] = up(z)
-
-    for copy in tokens.started + first.started + rest.started:
-        copy.wait_send()
+    send_down(0, c_buf, EARLY, 7)
+    in_dn[z] = down(c_buf, 7)
+
+    def own_up():
+        in_up[z] = up(x_buf, 7)
+
+    with_tokens(
+        tokens2, first2, x_two,
+        {
+            0: [functools.partial(preact_grad, c_buf, 0)],
+            1: [functools.partial(preact_grad, c_buf, 1)],
+            2: [functools.partial(preact_grad, c_buf, 2)],
+            3: [functools.partial(preact_grad, c_buf, 3)],
+            4: [functools.partial(send_up, 0, x_buf, 0, 2)],
+            5: [functools.partial(send_up, 0, x_buf, 2, 4), lambda: rest2.ready((0, 0))],
+            6: [functools.partial(send_up, 0, x_buf, 4, 7)],
+            7: [own_up],
+        },
+    )
+    send_down(1, c_two, 0, EARLY)
+    for n, roles in enumerate(ARRIVALS):
+        rest2.step(roles)
+        if n == 11:
+            rest2.from_sibling(0)
+            rest2.from_sibling(1)
+            preact_grad(c_two, 0)
+        elif n == 12:
+            preact_grad(c_two, 2)
+    rest2.from_sibling(2)
+    rest2.from_sibling(3)
+    preact_grad(c_two, 1)
+    preact_grad(c_two, 3)
+    send_up(1, x_two, 0, 7)
+    send_down(1, c_two, EARLY, 7)
+    opposite = lax.rem(z + 8, LANGS)
+    in_up[opposite] = up(x_two, 7)
+    in_dn[opposite] = down(c_two, 7)
 
     pairs[...] = jnp.zeros_like(pairs)
-
-    for inbox, out, send, recv in ((in_dn, out_dn, d_send, d_recv), (in_up, out_up, u_send, u_recv)):
-
-        @pl.loop(0, LANGS - 1)
-        def _(k):
-            source = lax.rem(z + LANGS - distance_of(k), LANGS)
-            grad_copy(out, inbox, k, source, send, recv).wait_recv()
+    targets_t = tgt[...].T
+    accept_t = acc[...].T
+
+    for sign, inbox in ((1, in_dn), (0, in_up)):
+        for number in range(2):
+
+            @pl.loop(0, 7)
+            def _(k):
+                grad_copy(sign, number, k, lax.rem(z + LANGS - distance_of(k, sign), LANGS)).wait_recv()
 
         @pl.loop(0, 2)
         def _(g):
@@ -417,8 +513,8 @@
     sends += exchange(st3, "lang", LANGS, z, s3_send, s3_recv)
     gram = jnp.sum(st3[...], axis=0)[:, :LANGS]
 
-    weights, new_targets = vaccinate(gram, tgt[...], acc[...])
-    nt_out[...] = new_targets
+    weights, cos_pairs = vaccinate(gram, targets_t, accept_t)
+    nt_out[...] = (1.0 - ema_rate) * tgt[...] + ema_rate * cos_pairs
     wv[...] = jnp.broadcast_to(weights, (LANGS, DS))
 
     for inbox, half in ((in_up, 0), (in_dn, 1)):
@@ -439,16 +535,24 @@
     for copy in sends:
         copy.wait_send()
 
-    @pl.loop(0, LANGS - 1)
-    def _(k):
-        grad_copy(out_dn, in_dn, k, z, d_send, d_recv).wait_send()
-        grad_copy(out_up, in_up, k, z, u_send, u_recv).wait_send()
+    for gather in (tokens, first, rest, tokens2, first2, rest2):
+        for copy in gather.started:
+            copy.wait_send()
+    for n in range(4):
+        first_leg(n).wait_send()
+        second_leg(n).wait_send()
+    for number in range(2):
+
+        @pl.loop(0, 7)
+        def _(k):
+            grad_copy(1, number, k, z).wait_send()
+            grad_copy(0, number, k, z).wait_send()
 
 
 def on_device(tokens, cotangent, lengths, up_weight, down_weight, targets, accept):
     bf16, f32 = jnp.bfloat16, jnp.float32
     dma = pltpu.SemaphoreType.DMA
-    any_space = pl.BlockSpec(memory_space=pl.ANY)
+    hbm = pl.BlockSpec(memory_space=pl.ANY)
     vmem = pl.BlockSpec(memory_space=pltpu.VMEM)
     return pl.pallas_call(
         kernel,
@@ -457,9 +561,11 @@
             jax.ShapeDtypeStruct((HID, DS), f32),
             jax.ShapeDtypeStruct((LANGS, LANGS), f32),
         ),
-        in_specs=[any_space] * 7,
+        in_specs=[hbm] * 7,
         out_specs=(vmem, vmem, vmem),
         scratch_shapes=[
+            pltpu.VMEM((2, 4, 4, ROWS, D), bf16),
+            pltpu.VMEM((2, 4, 4, ROWS, D), bf16),
             pltpu.VMEM((2, 4, 4, ROWS, D), bf16),
             pltpu.VMEM((2, 4, 4, ROWS, D), bf16),
             pltpu.VMEM((D, HID), bf16),
@@ -472,21 +578,20 @@
             pltpu.VMEM((LTOK, HID), bf16),
             pltpu.VMEM((HID, LTOK), bf16),
             pltpu.VMEM((HID, LTOK), bf16),
-            pltpu.VMEM((LANGS - 1, HID, DS), bf16),
-            pltpu.VMEM((LANGS - 1, HID, DS), bf16),
+            pltpu.VMEM((14, HID, DS), bf16),
+            pltpu.VMEM((14, HID, DS), bf16),
             pltpu.VMEM((LANGS, HID, DS), bf16),
             pltpu.VMEM((LANGS, HID, DS), bf16),
+            pltpu.VMEM((4, ROWS, HALF), bf16),
             pltpu.VMEM((256, 256), f32),
             pltpu.VMEM((NF, LANGS, 128), f32),
             pltpu.VMEM((NY, LANGS, 128), f32),
             pltpu.VMEM((LANGS, LANGS, 128), f32),
             pltpu.VMEM((LANGS, DS), f32),
             pltpu.VMEM((HID, DS), f32),
-            dma((6,)), dma((LANGS,)),
-            dma((20,)), dma((32,)), dma((4,)), dma((4,)),
-            dma((20,)), dma((32,)), dma((4,)), dma((4,)),
-            dma((20,)), dma((32,)), dma((4,)), dma((4,)),
-            dma((LANGS - 1,)), dma((LANGS - 1,)), dma((LANGS - 1,)), dma((LANGS - 1,)),
+            dma((6,)), dma((LANGS,)), dma((360,)),
+            dma((14,)), dma((14,)), dma((14,)), dma((14,)),
+            dma((4,)), dma((4,)), dma((4,)), dma((4,)),
             dma((NF,)), dma((NF,)), dma((NY,)), dma((NY,)), dma((LANGS,)), dma((LANGS,)),
         ],
         compiler_params=pltpu.CompilerParams(

time: 167 us -> 158 us (0.946)
  Pallas kernels: 162 us -> 154 us
    pallas_call x1, Pallas kernels: 162 us -> 154 us  [on_device(): pl.pallas_call(kernel, out_shape=(jax.ShapeDtypeStruct((DS, HID), f32), j...]
where the time goes in v5:
time: 158 us
  Pallas kernels  154 us (97%)
  local copies, waits for them, and re-layouts  2.9 us (2%)
    pallas_call x1, Pallas kernels, on_device(): pl.pallas_call(kernel, out_shape=(jax.ShapeDtypeStruct((DS, HID), f32), j...  154 us

profile of v5, /device:TPU:1, one launch (start us, length us, event | category | flops | bytes accessed | tf_op | source)
XLA Modules:
  0.0 157.7 jit_solution(15740769206658314725)
XLA Ops:
  0.6 154.2 %vaccine_step.1 = (f32[128,256]{1,0:T(8,128)}, f32[256,128]{1,0:T(8,128)}, f32[16,16]{1,0:T(8,128)}) custom-call(bf16[1,48,2048]{2,1,0:T(8,128)(2,1)} %tok_ref.1, bf16[1,48,2048]{2,1,0:T(8,128)(2,1)} %cot_ref.1, s32[1,12]{1,0:T(1,128)} %len_hbm.1, bf16[2048,256]{1,0:T(8,128)(2,1)} %wup_hbm.1, bf16[256,2048]{1,0:T(8,128)(2,1)} %wdn_hbm.1, f32[16,16]{1,0:T(8,128)} %tgt_hbm.1, ...), custom_call_target="tpu_custom_call" | custom-call | flops 6442450944 | bytes 4194304 | tf_op jit(solution)/shard_map/vaccine_step/pallas_call | solution.py:557
  154.8 0.0 copy-start
  154.8 1.6 %copy.13 = f32[128,256]{1,0:T(8,128)} copy(f32[128,256]{1,0:T(8,128)} %get-tuple-element.6) | data formatting | bytes 262144
  156.4 0.0 copy-done
  156.4 0.0 copy-start.1
  156.4 0.7 copy.14
  157.1 0.0 copy-done.1
  157.1 0.6 copy.15
Async XLA Ops:
  154.8 1.6 %copy-start = (f32[256,128]{1,0:T(8,128)S(1)}, f32[256,128]{1,0:T(8,128)}, u32[]{:S(2)}) copy-start(f32[256,128]{1,0:T(8,128)} %get-tuple-element.7) | copy-start | bytes 393220
  156.4 0.7 copy-start.1

commit v6 on v5

--- a/solution.py
+++ b/solution.py
@@ -29,7 +29,7 @@
     (0, 1), (0, 2), (1, 0), (2, 0), (0, 3), (1, 1), (2, 1), (1, 2), (2, 2),
     (1, 3), (2, 3), (3, 0), (3, 1), (3, 2), (3, 3),
 )
-EARLY = 4
+EARLY = 6
 
 
 class Plane:
@@ -127,9 +127,19 @@
             self.to_sibling(roles[0])
 
 
-def distance_of(k, sign):
-    m = 4 - (k + 1) // 2
-    return jnp.where(lax.rem(k + sign, 2) == 1, LANGS - m, m)
+NEAR = ((3, 2, 14, 1, 15, 5, 11, 12, 4, 13), (2, 14, 1, 15))
+COLUMN_ORDER = (2, 14, 1, 15, 0, 3, 12, 5)
+OWN_COLUMNS = 4
+COLUMN_OF = {d: i for i, d in enumerate(COLUMN_ORDER + tuple((d + 8) % 16 for d in COLUMN_ORDER))}
+
+
+def pick(k, values):
+    if isinstance(k, int):
+        return values[k]
+    found = jnp.int32(values[-1])
+    for i, value in enumerate(values[:-1]):
+        found = jnp.where(k == i, value, found)
+    return found
 
 
 def exchange(buf, axis, count, me, send, recv):
@@ -210,14 +220,14 @@
                 barrier, inc=1, device_id={axis: lax.rem(me + r, count)}, device_id_type=MESH
             )
 
-    def owner(k, sign):
-        return lax.rem(z + distance_of(k, sign), LANGS)
+    def owner(number, k):
+        return lax.rem(z + pick(k, NEAR[number]), LANGS)
 
     def columns(block):
         return pl.ds(pl.multiple_of(block * DS, DS), DS)
 
     def source_columns(k):
-        return columns(owner(k, 1) if k < 8 else lax.rem(owner(k - 8, 1) + 8, LANGS))
+        return columns(lax.rem(z + COLUMN_ORDER[k % 8] + 8 * (k // 8), LANGS))
 
     plane = Plane(x, y, core)
     tok, cot = tok_ref.at[0], cot_ref.at[0]
@@ -242,12 +252,13 @@
     early = EARLY * DS
 
     def gathers(number, own, x_ref, c_ref):
+        start_rest = early if number else 0
         made = []
         for n, (src, buf, start, width) in enumerate(
             (
                 (own, x_ref, 0, D),
                 (c_ref.at[0, 0, 0, :, pl.ds(0, early)], c_ref, 0, early),
-                (c_ref.at[0, 0, 0, :, pl.ds(early, D - early)], c_ref, early, D - early),
+                (c_ref.at[0, 0, 0, :, pl.ds(start_rest, D - start_rest)], c_ref, start_rest, D - start_rest),
             )
         ):
             base = (3 * number + n) * 60
@@ -255,7 +266,7 @@
             made.append(Gather(plane, src, buf, start, width, *parts))
         return made
 
-    tokens, first, rest = gathers(0, tok, x_buf, c_buf)
+    tokens, _, rest = gathers(0, tok, x_buf, c_buf)
     tokens2, first2, rest2 = gathers(1, x_two.at[0, 0, 0], x_two, c_two)
 
     def remote(src, dst, send, recv, to):
@@ -296,7 +307,6 @@
     kept = place < jnp.where(place < SEQ, here, after + SEQ)
     mine = c_buf[0, 0, 0].astype(jnp.float32)
     c_buf[0, 0, 0] = jnp.where(kept, mine, 0.0).astype(jnp.bfloat16)
-    first.ready((0, 0))
     first_leg(2).start()
     first_leg(3).start()
 
@@ -305,7 +315,7 @@
 
     @pl.loop(0, 8)
     def _(k):
-        low = owner(k, 1)
+        low = lax.rem(z + pick(k, COLUMN_ORDER), LANGS)
         wdn_t[pl.ds(pl.multiple_of(k * DS, DS), DS), :] = wdn[:, columns(low)].T
         high = lax.rem(low + 8, LANGS)
         wdn_t[pl.ds(pl.multiple_of(HALF + k * DS, DS), DS), :] = wdn[:, columns(high)].T
@@ -340,35 +350,36 @@
             preferred_element_type=jnp.float32,
         ).astype(jnp.bfloat16)
 
-    def up(x_ref, k):
+    def up(x_ref, block):
         return jnp.dot(
             p_t[...],
-            x_ref[:, :, :, :, columns(owner(k, 0))].reshape(LTOK, DS),
+            x_ref[:, :, :, :, columns(block)].reshape(LTOK, DS),
             preferred_element_type=jnp.float32,
         ).astype(jnp.bfloat16)
 
     def grad_copy(sign, number, k, source):
         out, inbox = (out_dn, in_dn) if sign else (out_up, in_up)
         send, recv = (d_send, d_recv) if sign else (u_send, u_recv)
-        index = number * 7 + k
+        index = number * len(NEAR[0]) + k
         return remote(
             out.at[index],
             inbox.at[lax.rem(source + 8 * number, LANGS)],
             send.at[index],
             recv.at[index],
-            owner(k, sign),
+            owner(number, k),
         )
 
     def send_down(number, c_ref, start, stop):
         @pl.loop(start, stop)
         def _(k):
-            out_dn[number * 7 + k] = down(c_ref, k)
+            place = pick(k, tuple(COLUMN_OF[d] for d in NEAR[number]))
+            out_dn[number * len(NEAR[0]) + k] = down(c_ref, place)
             grad_copy(1, number, k, z).start()
 
     def send_up(number, x_ref, start, stop):
         @pl.loop(start, stop)
         def _(k):
-            out_up[number * 7 + k] = up(x_ref, k)
+            out_up[number * len(NEAR[0]) + k] = up(x_ref, owner(number, k))
             grad_copy(0, number, k, z).start()
 
     def preact_grad(c_ref, pair):
@@ -383,7 +394,8 @@
     def with_tokens(gather_x, gather_c, x_ref, extra):
         for n, roles in enumerate(ARRIVALS):
             gather_x.step(roles)
-            gather_c.step(roles)
+            if gather_c is not None:
+                gather_c.step(roles)
             for piece in extra.get(n, ()):
                 piece()
             if n == 8:
@@ -408,8 +420,9 @@
         activate(x_ref, 1, 3)
         turn(h_t, 3, 3)
         turn(h_t, 9, 3)
-        for second in range(4):
-            gather_c.from_sibling(second)
+        if gather_c is not None:
+            for second in range(4):
+                gather_c.from_sibling(second)
 
     def begin_two():
         second_leg(0).wait_recv()
@@ -417,46 +430,54 @@
         tokens2.ready((0, 0))
 
     with_tokens(
-        tokens, first, x_buf,
+        tokens, None, x_buf,
         {
             4: [lambda: rest.ready((0, 0))],
             5: [lambda: forward(0), lambda: forward(1)],
             10: [lambda: forward(2), lambda: forward(3)],
         },
     )
-    send_down(0, c_buf, 0, EARLY)
     for n, roles in enumerate(ARRIVALS):
         rest.step(roles)
         if n == 8:
             begin_two()
+        elif n == 11:
+            rest.from_sibling(0)
+            rest.from_sibling(1)
+            preact_grad(c_buf, 0)
+        elif n == 12:
+            preact_grad(c_buf, 2)
     second_leg(2).wait_recv()
     second_leg(3).wait_recv()
     first2.ready((0, 0))
-    for second in range(4):
-        rest.from_sibling(second)
-    send_down(0, c_buf, EARLY, 7)
-    in_dn[z] = down(c_buf, 7)
+    rest.from_sibling(2)
+    rest.from_sibling(3)
+
+    def own_down():
+        in_dn[z] = down(c_buf, OWN_COLUMNS)
 
     def own_up():
-        in_up[z] = up(x_buf, 7)
+        in_up[z] = up(x_buf, z)
 
     with_tokens(
         tokens2, first2, x_two,
         {
-            0: [functools.partial(preact_grad, c_buf, 0)],
-            1: [functools.partial(preact_grad, c_buf, 1)],
-            2: [functools.partial(preact_grad, c_buf, 2)],
-            3: [functools.partial(preact_grad, c_buf, 3)],
-            4: [functools.partial(send_up, 0, x_buf, 0, 2)],
-            5: [functools.partial(send_up, 0, x_buf, 2, 4), lambda: rest2.ready((0, 0))],
-            6: [functools.partial(send_up, 0, x_buf, 4, 7)],
-            7: [own_up],
+            0: [functools.partial(send_down, 0, c_buf, 5, 8)],
+            1: [functools.partial(send_down, 0, c_buf, 8, 10)],
+            2: [functools.partial(send_down, 0, c_buf, 0, 5)],
+            3: [functools.partial(preact_grad, c_buf, 1)],
+            4: [functools.partial(preact_grad, c_buf, 3), lambda: rest2.ready((0, 0))],
+            5: [functools.partial(send_up, 0, x_buf, 5, 8)],
+            6: [functools.partial(send_up, 0, x_buf, 8, 10)],
+            7: [functools.partial(send_up, 0, x_buf, 0, 5), own_down],
         },
     )
-    send_down(1, c_two, 0, EARLY)
+    send_down(1, c_two, 0, 4)
     for n, roles in enumerate(ARRIVALS):
         rest2.step(roles)
-        if n == 11:
+        if n == 2:
+            own_up()
+        elif n == 11:
             rest2.from_sibling(0)
             rest2.from_sibling(1)
             preact_grad(c_two, 0)
@@ -466,11 +487,10 @@
     rest2.from_sibling(3)
     preact_grad(c_two, 1)
     preact_grad(c_two, 3)
-    send_up(1, x_two, 0, 7)
-    send_down(1, c_two, EARLY, 7)
+    send_up(1, x_two, 0, 4)
     opposite = lax.rem(z + 8, LANGS)
-    in_up[opposite] = up(x_two, 7)
-    in_dn[opposite] = down(c_two, 7)
+    in_up[opposite] = up(x_two, z)
+    in_dn[opposite] = down(c_two, OWN_COLUMNS)
 
     pairs[...] = jnp.zeros_like(pairs)
     targets_t = tgt[...].T
@@ -479,9 +499,10 @@
     for sign, inbox in ((1, in_dn), (0, in_up)):
         for number in range(2):
 
-            @pl.loop(0, 7)
+            @pl.loop(0, len(NEAR[number]))
             def _(k):
-                grad_copy(sign, number, k, lax.rem(z + LANGS - distance_of(k, sign), LANGS)).wait_recv()
+                source = lax.rem(z + LANGS - pick(k, NEAR[number]), LANGS)
+                grad_copy(sign, number, k, source).wait_recv()
 
         @pl.loop(0, 2)
         def _(g):
@@ -535,7 +556,7 @@
     for copy in sends:
         copy.wait_send()
 
-    for gather in (tokens, first, rest, tokens2, first2, rest2):
+    for gather in (tokens, rest, tokens2, first2, rest2):
         for copy in gather.started:
             copy.wait_send()
     for n in range(4):
@@ -543,7 +564,7 @@
         second_leg(n).wait_send()
     for number in range(2):
 
-        @pl.loop(0, 7)
+        @pl.loop(0, len(NEAR[number]))
         def _(k):
             grad_copy(1, number, k, z).wait_send()
             grad_copy(0, number, k, z).wait_send()

time: 158 us -> 150 us (0.949)
  Pallas kernels: 154 us -> 145 us
    pallas_call x1, Pallas kernels: 154 us -> 145 us  [on_device(): pl.pallas_call(kernel, out_shape=(jax.ShapeDtypeStruct((DS, HID), f32), j...]
where the time goes in v6:
time: 150 us; the launch traced here: 149 us
  Pallas kernels  145 us (97%)
  local copies, waits for them, and re-layouts  2.9 us (2%)
    pallas_call x1, Pallas kernels, on_device(): pl.pallas_call(kernel, out_shape=(jax.ShapeDtypeStruct((DS, HID), f32), j...  145 us

profile of v6, /device:TPU:1, one launch (start us, length us, event | category | flops | bytes accessed | tf_op | source)
XLA Modules:
  0.0 148.7 jit_solution(5103361359665262196)
XLA Ops:
  0.6 145.1 %vaccine_step.1 = (f32[128,256]{1,0:T(8,128)}, f32[256,128]{1,0:T(8,128)}, f32[16,16]{1,0:T(8,128)}) custom-call(bf16[1,48,2048]{2,1,0:T(8,128)(2,1)} %tok_ref.1, bf16[1,48,2048]{2,1,0:T(8,128)(2,1)} %cot_ref.1, s32[1,12]{1,0:T(1,128)} %len_hbm.1, bf16[2048,256]{1,0:T(8,128)(2,1)} %wup_hbm.1, bf16[256,2048]{1,0:T(8,128)(2,1)} %wdn_hbm.1, f32[16,16]{1,0:T(8,128)} %tgt_hbm.1, ...), custom_call_target="tpu_custom_call" | custom-call | flops 6442450944 | bytes 4194304 | tf_op jit(solution)/shard_map/vaccine_step/pallas_call | solution.py:578
  145.7 0.0 copy-start
  145.8 1.6 %copy.13 = f32[128,256]{1,0:T(8,128)} copy(f32[128,256]{1,0:T(8,128)} %get-tuple-element.6) | data formatting | bytes 262144
  147.4 0.0 copy-done
  147.4 0.0 copy-start.1
  147.4 0.7 copy.14
  148.0 0.0 copy-done.1
  148.1 0.6 copy.15
Async XLA Ops:
  145.7 1.6 %copy-start = (f32[256,128]{1,0:T(8,128)S(1)}, f32[256,128]{1,0:T(8,128)}, u32[]{:S(2)}) copy-start(f32[256,128]{1,0:T(8,128)} %get-tuple-element.7) | copy-start | bytes 393220
  147.4 0.7 copy-start.1

commit v7 on v6

--- a/solution.py
+++ b/solution.py
@@ -127,7 +127,7 @@
             self.to_sibling(roles[0])
 
 
-NEAR = ((3, 2, 14, 1, 15, 5, 11, 12, 4, 13), (2, 14, 1, 15))
+NEAR = ((5, 11, 12, 4, 13, 3, 2, 14, 1, 15), (2, 14, 1, 15))
 COLUMN_ORDER = (2, 14, 1, 15, 0, 3, 12, 5)
 OWN_COLUMNS = 4
 COLUMN_OF = {d: i for i, d in enumerate(COLUMN_ORDER + tuple((d + 8) % 16 for d in COLUMN_ORDER))}
@@ -343,19 +343,19 @@
             part = pl.ds(pl.multiple_of(i * 128, 128), 128)
             dst[:, part] = hp[part, :].T
 
-    def down(c_ref, k):
+    def product(grads_t, rows_ref, *blocks):
+        cols = [rows_ref[:, :, :, :, columns(b)].reshape(LTOK, DS) for b in blocks]
         return jnp.dot(
-            h_t[...],
-            c_ref[:, :, :, :, columns(k)].reshape(LTOK, DS),
+            grads_t[...],
+            cols[0] if len(cols) == 1 else jnp.concatenate(cols, axis=1),
             preferred_element_type=jnp.float32,
         ).astype(jnp.bfloat16)
 
-    def up(x_ref, block):
-        return jnp.dot(
-            p_t[...],
-            x_ref[:, :, :, :, columns(block)].reshape(LTOK, DS),
-            preferred_element_type=jnp.float32,
-        ).astype(jnp.bfloat16)
+    def down(c_ref, *places):
+        return product(h_t, c_ref, *places)
+
+    def up(x_ref, *blocks):
+        return product(p_t, x_ref, *blocks)
 
     def grad_copy(sign, number, k, source):
         out, inbox = (out_dn, in_dn) if sign else (out_up, in_up)
@@ -370,17 +370,31 @@
         )
 
     def send_down(number, c_ref, start, stop):
+        places = tuple(COLUMN_OF[d] for d in NEAR[number])
+
         @pl.loop(start, stop)
-        def _(k):
-            place = pick(k, tuple(COLUMN_OF[d] for d in NEAR[number]))
-            out_dn[number * len(NEAR[0]) + k] = down(c_ref, place)
-            grad_copy(1, number, k, z).start()
+        def _(pair):
+            k = 2 * pair
+            both = down(c_ref, pick(k, places), pick(k + 1, places))
+            for n in range(2):
+                out_dn[number * len(NEAR[0]) + k + n] = both[:, n * DS : (n + 1) * DS]
+                grad_copy(1, number, k + n, z).start()
 
     def send_up(number, x_ref, start, stop):
         @pl.loop(start, stop)
-        def _(k):
-            out_up[number * len(NEAR[0]) + k] = up(x_ref, owner(number, k))
-            grad_copy(0, number, k, z).start()
+        def _(pair):
+            k = 2 * pair
+            both = up(x_ref, owner(number, k), owner(number, k + 1))
+            for n in range(2):
+                out_up[number * len(NEAR[0]) + k + n] = both[:, n * DS : (n + 1) * DS]
+                grad_copy(0, number, k + n, z).start()
+
+    def preact_grad_group(c_ref, which, second):
+        hg = jnp.dot(
+            c_ref[which, second].reshape(192, D), wdn_t[...], preferred_element_type=jnp.float32
+        )
+        rows = pl.ds((which * 4 + second) * 192, 192)
+        hp[rows, :] = (hg * v_buf[rows, :]).astype(jnp.bfloat16)
 
     def preact_grad(c_ref, pair):
         which, second = pair // 2, 2 * (pair % 2)
@@ -391,7 +405,7 @@
         hp[rows, :] = (hg * v_buf[rows, :]).astype(jnp.bfloat16)
         turn(p_t, pair * 3, 3)
 
-    def with_tokens(gather_x, gather_c, x_ref, extra):
+    def with_tokens(gather_x, gather_c, x_ref, extra, following):
         for n, roles in enumerate(ARRIVALS):
             gather_x.step(roles)
             if gather_c is not None:
@@ -413,13 +427,18 @@
             elif n == 13:
                 gather_x.from_sibling(2)
                 activate(x_ref, 1, 2)
+        following.step(ARRIVALS[0])
+        activate(x_ref, 0, 3)
+        following.step(ARRIVALS[1])
         turn(h_t, 0, 3)
         turn(h_t, 6, 3)
-        activate(x_ref, 0, 3)
+        following.step(ARRIVALS[2])
         gather_x.from_sibling(3)
         activate(x_ref, 1, 3)
+        following.step(ARRIVALS[3])
         turn(h_t, 3, 3)
         turn(h_t, 9, 3)
+        following.step(ARRIVALS[4])
         if gather_c is not None:
             for second in range(4):
                 gather_c.from_sibling(second)
@@ -436,8 +455,11 @@
             5: [lambda: forward(0), lambda: forward(1)],
             10: [lambda: forward(2), lambda: forward(3)],
         },
+        rest,
     )
     for n, roles in enumerate(ARRIVALS):
+        if n < 5:
+            continue
         rest.step(roles)
         if n == 8:
             begin_two()
@@ -462,20 +484,23 @@
     with_tokens(
         tokens2, first2, x_two,
         {
-            0: [functools.partial(send_down, 0, c_buf, 5, 8)],
-            1: [functools.partial(send_down, 0, c_buf, 8, 10)],
-            2: [functools.partial(send_down, 0, c_buf, 0, 5)],
+            0: [functools.partial(send_down, 0, c_buf, 0, 2)],
+            1: [functools.partial(send_down, 0, c_buf, 2, 4)],
+            2: [functools.partial(send_down, 0, c_buf, 4, 5), own_down],
             3: [functools.partial(preact_grad, c_buf, 1)],
             4: [functools.partial(preact_grad, c_buf, 3), lambda: rest2.ready((0, 0))],
-            5: [functools.partial(send_up, 0, x_buf, 5, 8)],
-            6: [functools.partial(send_up, 0, x_buf, 8, 10)],
-            7: [functools.partial(send_up, 0, x_buf, 0, 5), own_down],
+            5: [functools.partial(send_up, 0, x_buf, 0, 2)],
+            6: [functools.partial(send_up, 0, x_buf, 2, 4)],
+            7: [functools.partial(send_up, 0, x_buf, 4, 5)],
         },
+        rest2,
     )
-    send_down(1, c_two, 0, 4)
+    send_down(1, c_two, 0, 2)
     for n, roles in enumerate(ARRIVALS):
+        if n < 5:
+            continue
         rest2.step(roles)
-        if n == 2:
+        if n == 6:
             own_up()
         elif n == 11:
             rest2.from_sibling(0)
@@ -483,11 +508,17 @@
             preact_grad(c_two, 0)
         elif n == 12:
             preact_grad(c_two, 2)
-    rest2.from_sibling(2)
+        elif n == 13:
+            rest2.from_sibling(2)
+            preact_grad_group(c_two, 0, 2)
+        elif n == 14:
+            preact_grad_group(c_two, 1, 2)
+    preact_grad_group(c_two, 0, 3)
+    turn(p_t, 3, 3)
     rest2.from_sibling(3)
-    preact_grad(c_two, 1)
-    preact_grad(c_two, 3)
-    send_up(1, x_two, 0, 4)
+    preact_grad_group(c_two, 1, 3)
+    turn(p_t, 9, 3)
+    send_up(1, x_two, 0, 2)
     opposite = lax.rem(z + 8, LANGS)
     in_up[opposite] = up(x_two, z)
     in_dn[opposite] = down(c_two, OWN_COLUMNS)

time: 150 us -> 145 us (0.967)
  Pallas kernels: 145 us -> 141 us
    pallas_call x1, Pallas kernels: 145 us -> 141 us  [on_device(): pl.pallas_call(kernel, out_shape=(jax.ShapeDtypeStruct((DS, HID), f32), j...]
where the time goes in v7:
time: 145 us
  Pallas kernels  141 us (97%)
  local copies, waits for them, and re-layouts  2.9 us (2%)
    pallas_call x1, Pallas kernels, on_device(): pl.pallas_call(kernel, out_shape=(jax.ShapeDtypeStruct((DS, HID), f32), j...  141 us
    unnamed x7, local copies, waits for them, and re-layouts  2.9 us

profile of v7, /device:TPU:1, one launch (start us, length us, event | category | flops | bytes accessed | tf_op | source)
XLA Modules:
  0.0 144.7 jit_solution(12427885272206926880)
XLA Ops:
  0.6 141.2 %vaccine_step.1 = (f32[128,256]{1,0:T(8,128)}, f32[256,128]{1,0:T(8,128)}, f32[16,16]{1,0:T(8,128)}) custom-call(bf16[1,48,2048]{2,1,0:T(8,128)(2,1)} %tok_ref.1, bf16[1,48,2048]{2,1,0:T(8,128)(2,1)} %cot_ref.1, s32[1,12]{1,0:T(1,128)} %len_hbm.1, bf16[2048,256]{1,0:T(8,128)(2,1)} %wup_hbm.1, bf16[256,2048]{1,0:T(8,128)(2,1)} %wdn_hbm.1, f32[16,16]{1,0:T(8,128)} %tgt_hbm.1, ...), custom_call_target="tpu_custom_call" | custom-call | flops 6442450944 | bytes 4194304 | tf_op jit(solution)/shard_map/vaccine_step/pallas_call | solution.py:609
  141.8 0.0 copy-start
  141.8 1.6 %copy.13 = f32[128,256]{1,0:T(8,128)} copy(f32[128,256]{1,0:T(8,128)} %get-tuple-element.6) | data formatting | bytes 262144
  143.4 0.0 copy-done
  143.4 0.0 copy-start.1
  143.4 0.7 copy.14
  144.1 0.0 copy-done.1
  144.1 0.6 copy.15
Async XLA Ops:
  141.8 1.6 %copy-start = (f32[256,128]{1,0:T(8,128)S(1)}, f32[256,128]{1,0:T(8,128)}, u32[]{:S(2)}) copy-start(f32[256,128]{1,0:T(8,128)} %get-tuple-element.7) | copy-start | bytes 393220
  143.4 0.7 copy-start.1

commit v8 on v7

--- a/solution.py
+++ b/solution.py
@@ -405,8 +405,10 @@
         hp[rows, :] = (hg * v_buf[rows, :]).astype(jnp.bfloat16)
         turn(p_t, pair * 3, 3)
 
-    def with_tokens(gather_x, gather_c, x_ref, extra, following):
+    def with_tokens(gather_x, gather_c, x_ref, start, extra, following):
         for n, roles in enumerate(ARRIVALS):
+            if n < start:
+                continue
             gather_x.step(roles)
             if gather_c is not None:
                 gather_c.step(roles)
@@ -449,7 +451,7 @@
         tokens2.ready((0, 0))
 
     with_tokens(
-        tokens, None, x_buf,
+        tokens, None, x_buf, 0,
         {
             4: [lambda: rest.ready((0, 0))],
             5: [lambda: forward(0), lambda: forward(1)],
@@ -461,17 +463,21 @@
         if n < 5:
             continue
         rest.step(roles)
-        if n == 8:
+        if n == 5:
             begin_two()
+        elif n == 9:
+            second_leg(2).wait_recv()
+            second_leg(3).wait_recv()
+            first2.ready((0, 0))
         elif n == 11:
             rest.from_sibling(0)
             rest.from_sibling(1)
             preact_grad(c_buf, 0)
         elif n == 12:
             preact_grad(c_buf, 2)
-    second_leg(2).wait_recv()
-    second_leg(3).wait_recv()
-    first2.ready((0, 0))
+        if n >= 10:
+            tokens2.step(ARRIVALS[n - 10])
+            first2.step(ARRIVALS[n - 10])
     rest.from_sibling(2)
     rest.from_sibling(3)
 
@@ -482,16 +488,18 @@
         in_up[z] = up(x_buf, z)
 
     with_tokens(
-        tokens2, first2, x_two,
+        tokens2, first2, x_two, 5,
         {
-            0: [functools.partial(send_down, 0, c_buf, 0, 2)],
-            1: [functools.partial(send_down, 0, c_buf, 2, 4)],
-            2: [functools.partial(send_down, 0, c_buf, 4, 5), own_down],
-            3: [functools.partial(preact_grad, c_buf, 1)],
-            4: [functools.partial(preact_grad, c_buf, 3), lambda: rest2.ready((0, 0))],
-            5: [functools.partial(send_up, 0, x_buf, 0, 2)],
-            6: [functools.partial(send_up, 0, x_buf, 2, 4)],
-            7: [functools.partial(send_up, 0, x_buf, 4, 5)],
+            5: [functools.partial(send_down, 0, c_buf, 0, 4)],
+            6: [
+                functools.partial(send_down, 0, c_buf, 4, 5),
+                own_down,
+                functools.partial(preact_grad, c_buf, 1),
+            ],
+            7: [functools.partial(preact_grad, c_buf, 3), lambda: rest2.ready((0, 0))],
+            8: [functools.partial(send_up, 0, x_buf, 0, 2)],
+            9: [functools.partial(send_up, 0, x_buf, 2, 4)],
+            10: [functools.partial(send_up, 0, x_buf, 4, 5)],
         },
         rest2,
     )

time: 145 us -> 148 us (1.021)
  Pallas kernels: 141 us -> 144 us
    pallas_call x1, Pallas kernels: 141 us -> 144 us  [on_device(): pl.pallas_call(kernel, out_shape=(jax.ShapeDtypeStruct((DS, HID), f32), j...]
where the time goes in v8:
time: 148 us
  Pallas kernels  144 us (97%)
  local copies, waits for them, and re-layouts  2.9 us (2%)
    pallas_call x1, Pallas kernels, on_device(): pl.pallas_call(kernel, out_shape=(jax.ShapeDtypeStruct((DS, HID), f32), j...  144 us

profile of v8, /device:TPU:1, one launch (start us, length us, event | category | flops | bytes accessed | tf_op | source)
XLA Modules:
  0.0 147.9 jit_solution(13677574393483690596)
XLA Ops:
  0.6 144.4 %vaccine_step.1 = (f32[128,256]{1,0:T(8,128)}, f32[256,128]{1,0:T(8,128)}, f32[16,16]{1,0:T(8,128)}) custom-call(bf16[1,48,2048]{2,1,0:T(8,128)(2,1)} %tok_ref.1, bf16[1,48,2048]{2,1,0:T(8,128)(2,1)} %cot_ref.1, s32[1,12]{1,0:T(1,128)} %len_hbm.1, bf16[2048,256]{1,0:T(8,128)(2,1)} %wup_hbm.1, bf16[256,2048]{1,0:T(8,128)(2,1)} %wdn_hbm.1, f32[16,16]{1,0:T(8,128)} %tgt_hbm.1, ...), custom_call_target="tpu_custom_call" | custom-call | flops 6442450944 | bytes 4194304 | tf_op jit(solution)/shard_map/vaccine_step/pallas_call | solution.py:617
  145.0 0.0 copy-start
  145.0 1.6 %copy.13 = f32[128,256]{1,0:T(8,128)} copy(f32[128,256]{1,0:T(8,128)} %get-tuple-element.6) | data formatting | bytes 262144
  146.6 0.0 copy-done
  146.6 0.0 copy-start.1
  146.6 0.7 copy.14
  147.3 0.0 copy-done.1
  147.3 0.6 copy.15
Async XLA Ops:
  145.0 1.6 %copy-start = (f32[256,128]{1,0:T(8,128)S(1)}, f32[256,128]{1,0:T(8,128)}, u32[]{:S(2)}) copy-start(f32[256,128]{1,0:T(8,128)} %get-tuple-element.7) | copy-start | bytes 393220
  146.6 0.7 copy-start.1

commit v9 on v7

--- a/solution.py
+++ b/solution.py
@@ -30,6 +30,7 @@
     (1, 3), (2, 3), (3, 0), (3, 1), (3, 2), (3, 3),
 )
 EARLY = 6
+LAG = 5
 
 
 class Plane:
@@ -408,8 +409,8 @@
     def with_tokens(gather_x, gather_c, x_ref, extra, following):
         for n, roles in enumerate(ARRIVALS):
             gather_x.step(roles)
-            if gather_c is not None:
-                gather_c.step(roles)
+            if gather_c is not None and n >= LAG:
+                gather_c.step(ARRIVALS[n - LAG])
             for piece in extra.get(n, ()):
                 piece()
             if n == 8:
@@ -427,18 +428,23 @@
             elif n == 13:
                 gather_x.from_sibling(2)
                 activate(x_ref, 1, 2)
-        following.step(ARRIVALS[0])
+        def next_step(n):
+            if gather_c is not None:
+                gather_c.step(ARRIVALS[len(ARRIVALS) - LAG + n])
+            following.step(ARRIVALS[n])
+
+        next_step(0)
         activate(x_ref, 0, 3)
-        following.step(ARRIVALS[1])
+        next_step(1)
         turn(h_t, 0, 3)
         turn(h_t, 6, 3)
-        following.step(ARRIVALS[2])
+        next_step(2)
         gather_x.from_sibling(3)
         activate(x_ref, 1, 3)
-        following.step(ARRIVALS[3])
+        next_step(3)
         turn(h_t, 3, 3)
         turn(h_t, 9, 3)
-        following.step(ARRIVALS[4])
+        next_step(4)
         if gather_c is not None:
             for second in range(4):
                 gather_c.from_sibling(second)
@@ -469,9 +475,12 @@
             preact_grad(c_buf, 0)
         elif n == 12:
             preact_grad(c_buf, 2)
-    second_leg(2).wait_recv()
-    second_leg(3).wait_recv()
-    first2.ready((0, 0))
+
+    def begin_first_two():
+        second_leg(2).wait_recv()
+        second_leg(3).wait_recv()
+        first2.ready((0, 0))
+
     rest.from_sibling(2)
     rest.from_sibling(3)
 
@@ -487,7 +496,7 @@
             0: [functools.partial(send_down, 0, c_buf, 0, 2)],
             1: [functools.partial(send_down, 0, c_buf, 2, 4)],
             2: [functools.partial(send_down, 0, c_buf, 4, 5), own_down],
-            3: [functools.partial(preact_grad, c_buf, 1)],
+            3: [functools.partial(preact_grad, c_buf, 1), begin_first_two],
             4: [functools.partial(preact_grad, c_buf, 3), lambda: rest2.ready((0, 0))],
             5: [functools.partial(send_up, 0, x_buf, 0, 2)],
             6: [functools.partial(send_up, 0, x_buf, 2, 4)],

time: 145 us -> 144 us (level)
  no operation moved by 1% of the time
where the time goes in v9:
time: 144 us
  Pallas kernels  140 us (97%)
  local copies, waits for them, and re-layouts  2.9 us (2%)
    pallas_call x1, Pallas kernels, on_device(): pl.pallas_call(kernel, out_shape=(jax.ShapeDtypeStruct((DS, HID), f32), j...  140 us
    unnamed x7, local copies, waits for them, and re-layouts  2.9 us

profile of v9, /device:TPU:1, one launch (start us, length us, event | category | flops | bytes accessed | tf_op | source)
XLA Modules:
  0.0 143.8 jit_solution(10240318418846403346)
XLA Ops:
  0.6 140.3 %vaccine_step.1 = (f32[128,256]{1,0:T(8,128)}, f32[256,128]{1,0:T(8,128)}, f32[16,16]{1,0:T(8,128)}) custom-call(bf16[1,48,2048]{2,1,0:T(8,128)(2,1)} %tok_ref.1, bf16[1,48,2048]{2,1,0:T(8,128)(2,1)} %cot_ref.1, s32[1,12]{1,0:T(1,128)} %len_hbm.1, bf16[2048,256]{1,0:T(8,128)(2,1)} %wup_hbm.1, bf16[256,2048]{1,0:T(8,128)(2,1)} %wdn_hbm.1, f32[16,16]{1,0:T(8,128)} %tgt_hbm.1, ...), custom_call_target="tpu_custom_call" | custom-call | flops 6442450944 | bytes 4194304 | tf_op jit(solution)/shard_map/vaccine_step/pallas_call | solution.py:618
  140.9 0.0 copy-start
  140.9 1.6 %copy.13 = f32[128,256]{1,0:T(8,128)} copy(f32[128,256]{1,0:T(8,128)} %get-tuple-element.6) | data formatting | bytes 262144
  142.5 0.0 copy-done
  142.5 0.0 copy-start.1
  142.5 0.7 copy.14
  143.2 0.0 copy-done.1
  143.2 0.6 copy.15
Async XLA Ops:
  140.9 1.6 %copy-start = (f32[256,128]{1,0:T(8,128)S(1)}, f32[256,128]{1,0:T(8,128)}, u32[]{:S(2)}) copy-start(f32[256,128]{1,0:T(8,128)} %get-tuple-element.7) | copy-start | bytes 393220
  142.5 0.7 copy-start.1
